TPU v7x, 128 devices: a whole 4x4x4 slice. The times are simulated.
128 devices in a mesh: pb: 8 (over z_hi, y), ka: 16 (over z_lo, x, core).
Axes of the slice: x: 4, y: 4, z: 4 (z_hi: 2, z_lo: 2; z = z_hi * 2 + z_lo), core: 2. Of those that a mesh axis runs over, the one named last changes fastest.
Arguments:
- queries: bfloat16 [8192, 1024], P(('pb', 'ka')), may hold values from -12 to 12
- key_rows: bfloat16 [8192, 1024], P(('ka', 'pb')), may hold values from -6 to 6
- value_rows: bfloat16 [8192, 1024], P(('ka', 'pb')), may hold values from -6 to 6
- output_rows: bfloat16 [8192, 1024], P(('pb', 'ka')), may hold values from -3 to 3
- grad_out: bfloat16 [8192, 1024], P(('pb', 'ka')), may hold values from -6 to 6
- log_sums: float32 [8192, 16], P(('pb', 'ka')), as said below
Outputs:
- grad_queries: float32 [8192, 1024], P(('pb', 'ka'))
- grad_keys: float32 [8192, 1024], P(('ka', 'pb'))
- grad_values: float32 [8192, 1024], P(('ka', 'pb'))
Inputs may be any that keep to these rules, and one draw needn't show every extreme that they name: log_sums lies within half a unit of log(8192) + 2.
All inputs are finite; a program needn't handle non-finite values.
Results may differ from a plain program's by a relative error of at most 0.004.
Values may be sent and summed in bfloat16 or wider, within the bound.
A program may use at most 128 MiB of HBM per device.

v0:
```python
import jax
import jax.numpy as jnp
from jax import lax
from jax.sharding import PartitionSpec as P


def row_products(grad_rows, out_rows, head_count):
    row_count = grad_rows.shape[0]
    product = grad_rows.astype(jnp.float32) * out_rows.astype(jnp.float32)
    return jnp.sum(product.reshape(row_count, head_count, -1), axis=-1)


def group_terms(
    query_block,
    grad_block,
    key_block,
    value_block,
    sums_rows,
    delta_rows,
    group_index,
    per_group,
    head_size,
):
    first = group_index * per_group * head_size
    last = first + per_group * head_size
    query_group = query_block[:, first:last].reshape(query_block.shape[0], per_group, head_size)
    grad_group = grad_block[:, first:last].reshape(grad_block.shape[0], per_group, head_size)
    key_group = key_block[:, first:last].reshape(key_block.shape[0], per_group, head_size)
    value_group = value_block[:, first:last].reshape(value_block.shape[0], per_group, head_size)
    sums_group = sums_rows[:, group_index * per_group : (group_index + 1) * per_group].T
    delta_group = delta_rows[:, group_index * per_group : (group_index + 1) * per_group].T
    scaling = head_size ** (-0.5)
    scores = (
        jnp.einsum("qhd,khd->hqk", query_group, key_group, preferred_element_type=jnp.float32)
        * scaling
    )
    probs = jnp.exp(scores - sums_group[:, :, None])
    grad_probs = jnp.einsum(
        "qhd,khd->hqk", grad_group, value_group, preferred_element_type=jnp.float32
    )
    grad_scores = (probs * (grad_probs - delta_group[:, :, None])).astype(jnp.bfloat16)
    probs_low = probs.astype(jnp.bfloat16)
    return (probs_low, grad_scores, query_group, grad_group, key_group, scaling)


def key_side_terms(probs_low, grad_scores, query_group, grad_group, scaling):
    key_count = probs_low.shape[2]
    grad_keys = (
        jnp.einsum("hqk,qhd->khd", grad_scores, query_group, preferred_element_type=jnp.float32)
        * scaling
    )
    grad_values = jnp.einsum(
        "hqk,qhd->khd", probs_low, grad_group, preferred_element_type=jnp.float32
    )
    return (grad_keys.reshape(key_count, -1), grad_values.reshape(key_count, -1))


def query_side_terms(grad_scores, key_group, scaling):
    query_count = grad_scores.shape[1]
    grad_queries = (
        jnp.einsum("hqk,khd->qhd", grad_scores, key_group, preferred_element_type=jnp.float32)
        * scaling
    )
    return grad_queries.reshape(query_count, -1)


def shards(queries, key_rows, value_rows, output_rows, grad_out, log_sums):
    head_count = log_sums.shape[1]
    model_width = queries.shape[1]
    head_size = model_width // head_count
    per_group = min(head_count, max(1, 128 // head_size))
    group_total = head_count // per_group
    key_block, value_block = (
        lax.all_gather(key_rows, "pb", axis=0, tiled=True),
        lax.all_gather(value_rows, "pb", axis=0, tiled=True),
    )
    query_block, grad_block, out_block = (
        lax.all_gather(queries, "ka", axis=0, tiled=True),
        lax.all_gather(grad_out, "ka", axis=0, tiled=True),
        lax.all_gather(output_rows, "ka", axis=0, tiled=True),
    )
    sums_rows = lax.all_gather(log_sums, "ka", axis=0, tiled=True)
    delta_rows = row_products(grad_block, out_block, head_count)
    query_parts = []
    key_parts = []
    value_parts = []
    for group_index in range(group_total):
        probs_low, grad_scores, query_group, grad_group, key_group, scaling = group_terms(
            query_block,
            grad_block,
            key_block,
            value_block,
            sums_rows,
            delta_rows,
            group_index,
            per_group,
            head_size,
        )
        query_parts.append(query_side_terms(grad_scores, key_group, scaling))
        grad_keys, grad_values = key_side_terms(
            probs_low, grad_scores, query_group, grad_group, scaling
        )
        key_parts.append(grad_keys)
        value_parts.append(grad_values)
    query_partial = jnp.concatenate(query_parts, axis=1)
    key_partial = jnp.concatenate(key_parts, axis=1)
    value_partial = jnp.concatenate(value_parts, axis=1)
    grad_keys, grad_values = (
        lax.psum_scatter(key_partial, "pb", scatter_dimension=0, tiled=True),
        lax.psum_scatter(value_partial, "pb", scatter_dimension=0, tiled=True),
    )
    grad_queries = lax.psum_scatter(query_partial, "ka", scatter_dimension=0, tiled=True)
    return (grad_queries, grad_keys, grad_values)


def solution(mesh):
    placed = (
        P(("pb", "ka"), None),
        P(("ka", "pb"), None),
        P(("ka", "pb"), None),
        P(("pb", "ka"), None),
        P(("pb", "ka"), None),
        P(("pb", "ka"), None),
    )
    return jax.shard_map(
        shards,
        mesh=mesh,
        in_specs=placed,
        out_specs=(P(("pb", "ka"), None), P(("ka", "pb"), None), P(("ka", "pb"), None)),
        check_vma=False,
    )
```

profile of v0, /device:TPU:1, one launch (start us, length us, event | category | flops | bytes accessed | tf_op | source)
XLA Modules:
  0.0 527.1 jit_solution(17329162622286902601)
XLA Ops:
  10.6 22.1 %all-gather = f32[16,64,16]{1,2,0:T(8,128)S(1)} all-gather(f32[1,64,16]{1,2,0:T(8,128)} %bitcast.293), channel_id=1, replica_groups=mesh['pb'=8,'ka'=16] {'ka'}, dimensions={0}, use_global_device_ids=true | all-gather | bytes 69632 | tf_op jit(solution)/shard_map/all_gather | solution.py:82
  33.4 26.7 %all-gather.9.cloned.1.call-done = bf16[512,1024]{1,0:T(8,128)(2,1)} async-done(((bf16[64,1024]{1,0:T(8,128)(2,1)}), bf16[512,1024]{1,0:T(8,128)(2,1)}) %all-gather.9.cloned.1.call-update) | async-done | bytes 1048592 | tf_op jit(solution)/shard_map/all_gather | solution.py:74
  61.6 46.9 %all-gather.13.cloned.1.call-done = bf16[512,1024]{1,0:T(8,128)(2,1)} async-done(((bf16[64,1024]{1,0:T(8,128)(2,1)}), bf16[512,1024]{1,0:T(8,128)(2,1)}) %all-gather.13.cloned.1.call-update) | async-done | bytes 1048592 | tf_op jit(solution)/shard_map/all_gather | solution.py:75
  121.4 22.9 %all-gather.7.cloned.1.call-done = bf16[1024,1024]{1,0:T(8,128)(2,1)} async-done(((bf16[64,1024]{1,0:T(8,128)(2,1)}), bf16[1024,1024]{1,0:T(8,128)(2,1)}) %all-gather.7.cloned.1.call-update) | async-done | bytes 2097168 | tf_op jit(solution)/shard_map/all_gather | solution.py:78
  150.0 30.0 %all-gather.11.cloned.1.call-done = bf16[1024,1024]{1,0:T(8,128)(2,1)} async-done(((bf16[64,1024]{1,0:T(8,128)(2,1)}), bf16[1024,1024]{1,0:T(8,128)(2,1)}) %all-gather.11.cloned.1.call-update) | async-done | bytes 2097168 | tf_op jit(solution)/shard_map/all_gather | solution.py:79
  179.9 3.0 fusion.32
  196.6 2.6 copy.121
  199.1 16.4 %all-gather.15.cloned.1.call-done = bf16[1024,1024]{1,0:T(8,128)(2,1)} async-done(((bf16[64,1024]{1,0:T(8,128)(2,1)}), bf16[1024,1024]{1,0:T(8,128)(2,1)}) %all-gather.15.cloned.1.call-update) | async-done | bytes 2097168 | tf_op jit(solution)/shard_map/all_gather | solution.py:80
  215.5 3.9 copy.122
  219.5 2.6 bitcast_reduce_fusion
  302.1 3.6 multiply_convert_fusion.4
  310.0 3.7 multiply_convert_fusion.3
  318.0 3.6 multiply_convert_fusion.2
  326.0 3.0 multiply_convert_fusion.1
  331.7 3.1 multiply_convert_fusion
  348.5 3.3 convolution_multiply_fusion.6
  354.6 2.2 copy.153
  356.8 3.1 convolution_multiply_fusion.4
  362.0 2.5 convolution_multiply_fusion.3
  364.5 2.2 copy.155
  366.7 3.2 convolution_multiply_fusion.2
  375.6 3.2 convolution_multiply_fusion
  387.9 66.6 %reduce-scatter.6.cloned.1.call-done = f32[64,1024]{1,0:T(8,128)} async-done(((f32[512,1024]{1,0:T(8,128)}), f32[64,1024]{1,0:T(8,128)}) %reduce-scatter.6.cloned.1.call-update) | async-done | bytes 262160 | tf_op jit(solution)/shard_map/reduce_scatter | solution.py:109
  454.5 65.8 %reduce-scatter.4.cloned.1.call-done = f32[64,1024]{1,0:T(8,128)} async-done(((f32[1024,1024]{1,0:T(8,128)}), f32[64,1024]{1,0:T(8,128)}) %reduce-scatter.4.cloned.1.call-update) | async-done | bytes 262160 | tf_op jit(solution)/shard_map/reduce_scatter | solution.py:112
  (239 shorter events, 166.3 us)
Async XLA Ops:
  7.2 52.9 %all-gather.9.cloned.1.call-start = ((), (), s32[]{:S(2)}) async-start(), calls=%async_computation.4 | async-start | bytes 1179648 | tf_op jit(solution)/shard_map/all_gather | solution.py:74
  7.9 100.6 %all-gather.13.cloned.1.call-start = ((), (), s32[]{:S(2)}) async-start(), calls=%async_computation.6 | async-start | bytes 1179648 | tf_op jit(solution)/shard_map/all_gather | solution.py:75
  8.6 135.6 %all-gather.7.cloned.1.call-start = ((), (), s32[]{:S(2)}) async-start(), calls=%async_computation.3 | async-start | bytes 2228224 | tf_op jit(solution)/shard_map/all_gather | solution.py:78
  9.4 170.5 %all-gather.11.cloned.1.call-start = ((), (), s32[]{:S(2)}) async-start(), calls=%async_computation.5 | async-start | bytes 2228224 | tf_op jit(solution)/shard_map/all_gather | solution.py:79
  10.0 205.6 %all-gather.15.cloned.1.call-start = ((), (), s32[]{:S(2)}) async-start(), calls=%async_computation.7 | async-start | bytes 2228224 | tf_op jit(solution)/shard_map/all_gather | solution.py:80
  10.5 377.4 %reduce-scatter.8.cloned.1.call-start = ((), (), s32[]{:S(2)}) async-start(), calls=%async_computation.10 | async-start | bytes 2359296 | tf_op jit(solution)/shard_map/reduce_scatter | solution.py:110
  179.9 16.6 %copy-start.15 = (bf16[1024,1024]{1,0:T(8,128)(2,1)S(1)}, bf16[1024,1024]{1,0:T(8,128)(2,1)}, u32[]{:S(2)}) copy-start(bf16[1024,1024]{1,0:T(8,128)(2,1)} %all-gather.11.cloned.1.call-done) | copy-start | bytes 6291460
  199.1 20.4 %copy-start.16 = (bf16[1024,1024]{0,1:T(8,128)(2,1)S(1)}, bf16[1024,1024]{0,1:T(8,128)(2,1)}, u32[]{:S(2)}) copy-start(bf16[1024,1024]{0,1:T(8,128)(2,1)} %copy.121) | copy-start | bytes 6291460
  301.7 152.7 %reduce-scatter.6.cloned.1.call-start = ((), (), s32[]{:S(2)}) async-start(), calls=%async_computation.9 | async-start | bytes 2359296 | tf_op jit(solution)/shard_map/reduce_scatter | solution.py:109
  318.0 7.9 %copy-start.18 = (bf16[1024,128]{0,1:T(8,128)(2,1)S(1)}, bf16[1024,128]{0,1:T(8,128)(2,1)}, u32[]{:S(2)}) copy-start(bf16[1024,128]{0,1:T(8,128)(2,1)} %copy.145) | copy-start | bytes 786436
  336.2 11.4 %copy-start.40 = (bf16[512,128]{0,1:T(8,128)(2,1)S(1)}, bf16[512,128]{0,1:T(8,128)(2,1)}, u32[]{:S(2)}) copy-start(bf16[512,128]{0,1:T(8,128)(2,1)} %copy.117) | copy-start | bytes 393220
  347.5 5.6 %copy-start.38 = (bf16[512,128]{0,1:T(8,128)(2,1)S(1)}, bf16[512,128]{0,1:T(8,128)(2,1)}, u32[]{:S(2)}) copy-start(bf16[512,128]{0,1:T(8,128)(2,1)} %copy.128) | copy-start | bytes 393220
  347.5 172.7 %reduce-scatter.4.cloned.1.call-start = ((), (), s32[]{:S(2)}) async-start(), calls=%async_computation.8 | async-start | bytes 4456448 | tf_op jit(solution)/shard_map/reduce_scatter | solution.py:112
  348.3 8.5 %copy-start.37 = (bf16[512,128]{0,1:T(8,128)(2,1)S(1)}, bf16[512,128]{0,1:T(8,128)(2,1)}, u32[]{:S(2)}) copy-start(bf16[512,128]{0,1:T(8,128)(2,1)} %copy.132) | copy-start | bytes 393220
  354.6 7.4 %copy-start.10 = (bf16[2,1024,512]{2,1,0:T(8,128)(2,1)S(1)}, bf16[2,1024,512]{2,1,0:T(8,128)(2,1)}, u32[]{:S(2)}) copy-start(bf16[2,1024,512]{2,1,0:T(8,128)(2,1)} %copy-done.9) | copy-start | bytes 6291460
  354.6 12.1 %copy-start.36 = (bf16[512,128]{0,1:T(8,128)(2,1)S(1)}, bf16[512,128]{0,1:T(8,128)(2,1)}, u32[]{:S(2)}) copy-start(bf16[512,128]{0,1:T(8,128)(2,1)} %copy.140) | copy-start | bytes 393220
  359.9 12.0 %copy-start.35 = (bf16[512,128]{0,1:T(8,128)(2,1)S(1)}, bf16[512,128]{0,1:T(8,128)(2,1)}, u32[]{:S(2)}) copy-start(bf16[512,128]{0,1:T(8,128)(2,1)} %copy.144) | copy-start | bytes 393220
  364.5 7.4 %copy-start.13 = (bf16[2,1024,512]{2,1,0:T(8,128)(2,1)S(1)}, bf16[2,1024,512]{2,1,0:T(8,128)(2,1)}, u32[]{:S(2)}) copy-start(bf16[2,1024,512]{2,1,0:T(8,128)(2,1)} %copy-done.12) | copy-start | bytes 6291460
  373.5 9.2 %copy-start.29 = (f32[1024,128]{1,0:T(8,128)S(1)}, f32[1024,128]{1,0:T(8,128)}, u32[]{:S(2)}) copy-start(f32[1024,128]{1,0:T(8,128)} %copy.153) | copy-start | bytes 1572868
  373.5 10.0 %copy-start.30 = (f32[1024,128]{1,0:T(8,128)S(1)}, f32[1024,128]{1,0:T(8,128)}, u32[]{:S(2)}) copy-start(f32[1024,128]{1,0:T(8,128)} %copy.154) | copy-start | bytes 1572868
  375.6 8.8 %copy-start.31 = (f32[1024,128]{1,0:T(8,128)S(1)}, f32[1024,128]{1,0:T(8,128)}, u32[]{:S(2)}) copy-start(f32[1024,128]{1,0:T(8,128)} %copy.155) | copy-start | bytes 1572868
  375.6 9.7 %copy-start.32 = (f32[1024,128]{1,0:T(8,128)S(1)}, f32[1024,128]{1,0:T(8,128)}, u32[]{:S(2)}) copy-start(f32[1024,128]{1,0:T(8,128)} %copy.156) | copy-start | bytes 1572868
  380.9 5.2 copy-start.33
  380.9 6.1 %copy-start.34 = (f32[1024,128]{1,0:T(8,128)S(1)}, f32[1024,128]{1,0:T(8,128)}, u32[]{:S(2)}) copy-start(f32[1024,128]{1,0:T(8,128)} %copy.158) | copy-start | bytes 1572868
  (38 other events, 109.3 us)
Sparse Core Ops, SparseCore 0:
  10.3 49.7 all-gather.8
  62.4 46.0 all-gather.12
  110.2 33.9 all-gather.6
  145.8 34.0 all-gather.10
  181.5 34.0 all-gather.14
  301.9 73.6 reduce-scatter.7
  380.4 74.0 reduce-scatter.5
  457.5 62.7 reduce-scatter.3
where the time goes:
time: 532 us; the launch traced here: 527 us
  waiting for transfers between devices  278 us (52%)
  local copies, waits for them, and re-layouts  136 us (26%)
  matrix products  73.2 us (14%)
  blocking collectives  22.1 us (4%)
  between operations  14.7 us (3%)
    reduce_scatter x1, waiting for transfers between devices, shards(): lax.psum_scatter(key_partial, 'pb', scatter_dimension=0, tiled=True)  66.6 us
    reduce_scatter x1, waiting for transfers between devices, shards(): lax.psum_scatter(query_partial, 'ka', scatter_dimension=0, tiled=True)  65.8 us
    unnamed x130, local copies, waits for them, and re-layouts  48.4 us
    all_gather x1, waiting for transfers between devices, shards(): lax.all_gather(value_rows, 'pb', axis=0, tiled=True)  46.9 us
    all_gather x1, waiting for transfers between devices, shards(): lax.all_gather(grad_out, 'ka', axis=0, tiled=True)  30 us
    all_gather x1, waiting for transfers between devices, shards(): lax.all_gather(key_rows, 'pb', axis=0, tiled=True)  26.7 us
    all_gather x1, waiting for transfers between devices, shards(): lax.all_gather(queries, 'ka', axis=0, tiled=True)  22.9 us
    all_gather x1, blocking collectives, shards(): sums_rows = lax.all_gather(log_sums, 'ka', axis=0, tiled=True)  22.1 us
  transfers between devices with their start and end apart: 8, of which 7 were waited for; matrix products, arithmetic and copies ran while one was open for 23% of the time, Pallas kernels for 0%

commit v1 on v0

v1 whole, which is shorter than its diff:
```python
import functools

import jax
import jax.numpy as jnp
from jax import lax
from jax.experimental import pallas as pl
from jax.experimental.pallas import tpu as pltpu
from jax.sharding import PartitionSpec as P

BF = jnp.bfloat16
F32 = jnp.float32
MESH = pl.DeviceIdType.MESH

ROWS = 64
PAIR = 128
HEAD = 64
GROUP = 8
RING = 4
CHUNK = GROUP * ROWS
SIDE = 2 * ROWS + 16
OFFSETS = (0, 1, -1, 2)
SLOT_AT = {0: 0, -1: 1, 1: 2, 2: 3}
STEPS = RING * RING


def dot_nn(a, b):
    return jnp.dot(a, b, preferred_element_type=F32)


def dot_nt(a, b):
    return lax.dot_general(a, b, (((1,), (1,)), ((), ())), preferred_element_type=F32)


def split3(value):
    high = value.astype(BF)
    rest = value - high.astype(F32)
    mid = rest.astype(BF)
    low = (rest - mid.astype(F32)).astype(BF)
    return high, mid, low


def select_rows(matrix, value):
    high, mid, low = split3(value)
    return dot_nt(matrix, high) + dot_nt(matrix, mid) + dot_nt(matrix, low)


def kernel(
    q_in, k_in, v_in, o_in, g_in, sums_in,
    dq_out, dk_out, dv_out,
    stage_q, stage_k, qbuf, kbuf, qm, gm, kt, terms,
    dq_acc, dk_acc, dv_acc, kv_send, kv_recv, q_send, q_recv,
    back_kv, back_q, home_kv, home_q,
    in_send, in_recv, ring_send, ring_recv, sum_send, sum_recv, out_send, out_recv,
):
    pb = lax.axis_index("pb")
    ka = lax.axis_index("ka")
    y = lax.rem(pb, 4)
    z_hi = pb // 4
    me = lax.rem(ka, 8)
    z_lo = ka // 8
    z = z_hi * 2 + z_lo

    def along_x(offset):
        return (pb, z_lo * 8 + lax.rem(me + (offset + 8), 8))

    def along_y(offset):
        return (z_hi * 4 + lax.rem(y + (offset + 4), 4), ka)

    def along_z(offset):
        there = lax.rem(z + (offset + 4), 4)
        return ((there // 2) * 4 + y, lax.rem(there, 2) * 8 + me)

    barrier = pltpu.get_barrier_semaphore()
    for peer in (
        [along_x(d) for d in range(1, GROUP)]
        + [along_y(d) for d in (1, 2, 3)]
        + [along_z(d) for d in (1, 2, 3)]
    ):
        pl.semaphore_signal(barrier, inc=1, device_id=peer, device_id_type=MESH)

    def remote(src, dst, send, recv, peer):
        return pltpu.make_async_remote_copy(
            src_ref=src, dst_ref=dst, send_sem=send, recv_sem=recv,
            device_id=peer, device_id_type=MESH,
        )

    def in_copy(side, d):
        stage, buf = ((stage_q, qbuf), (stage_k, kbuf))[side]
        return remote(
            stage.at[lax.rem(me + d, GROUP)], buf.at[0, d],
            in_send.at[side, d], in_recv.at[side, d], along_x(d),
        )

    def ring_copy(side, offset):
        buf, along = ((qbuf, along_y), (kbuf, along_z))[side]
        slot = SLOT_AT[offset]
        return remote(
            buf.at[0], buf.at[slot],
            ring_send.at[side, slot], ring_recv.at[side, slot], along(offset),
        )

    def forward_copy(side, half):
        buf, along = ((qbuf, along_y), (kbuf, along_z))[side]
        part = pl.ds(half * (GROUP // 2), GROUP // 2)
        index = 3 if half == 0 else 0
        return remote(
            buf.at[1 + half, part], buf.at[3, part],
            ring_send.at[side, index], ring_recv.at[side, index], along((-1, 1)[half]),
        )

    def kv_copy(slot):
        return remote(
            kv_send.at[slot - 1], kv_recv.at[slot - 1],
            sum_send.at[0, slot], sum_recv.at[0, slot], along_z(OFFSETS[slot]),
        )

    def q_copy(slot):
        return remote(
            q_send.at[slot - 1], q_recv.at[slot - 1],
            sum_send.at[1, slot], sum_recv.at[1, slot], along_y(OFFSETS[slot]),
        )

    def out_copy(side, d):
        back, home = ((back_q, home_q), (back_kv, home_kv))[side]
        return remote(
            back.at[d], home.at[d],
            out_send.at[side, d], out_recv.at[side, d], along_x(-d),
        )

    for p in range(GROUP):
        cols = slice(p * PAIR, (p + 1) * PAIR)
        stage_q[p, 0:ROWS] = q_in[:, cols]
        stage_q[p, ROWS : 2 * ROWS] = g_in[:, cols]
        stage_k[p, 0:ROWS] = k_in[:, cols]
        stage_k[p, ROWS : 2 * ROWS] = v_in[:, cols]

    product = g_in[...].astype(F32) * o_in[...].astype(F32)
    product = jnp.concatenate([product, product], axis=0)
    sums = jnp.concatenate([sums_in[...], sums_in[...]], axis=0)
    count = 16 * GROUP

    def row_of(shape):
        return lax.broadcasted_iota(jnp.int32, shape, 0)

    def col_of(shape):
        return lax.broadcasted_iota(jnp.int32, shape, 1)

    def pick(width, first, per_head):
        row, col = row_of((count, width)), col_of((count, width))
        kind = row % 4
        head = 2 * (row // 16) + kind - first
        hit = (row % 16 < 12) & (kind >= first) & (kind < first + 2) & (col // per_head == head)
        return jnp.where(hit, 1.0, 0.0).astype(BF)

    value = select_rows(pick(GROUP * PAIR, 2, HEAD), product) + select_rows(pick(16, 0, 1), sums)
    high = value.astype(BF).astype(F32)
    mid = (value - high).astype(BF).astype(F32)
    low = value - high - mid
    row, col = row_of((count, PAIR)), col_of((count, PAIR))
    third = (row % 16) // 4
    value = jnp.where(third == 0, high, jnp.where(third == 1, mid, low))
    value = jnp.where(col // ROWS == (row // 16 + me) % 2, value, 0.0).astype(BF)
    for p in range(GROUP):
        stage_q[p, 2 * ROWS : SIDE] = value[16 * p : 16 * (p + 1)]

    pl.semaphore_wait(barrier, 13)
    for d in (4, 5, 3, 2, 6, 7, 1):
        in_copy(1, d).start()
        in_copy(0, d).start()
    kbuf[0, 0] = stage_k[me]
    qbuf[0, 0] = stage_q[me]
    dq_acc[...] = jnp.zeros_like(dq_acc)
    dk_acc[...] = jnp.zeros_like(dk_acc)
    dv_acc[...] = jnp.zeros_like(dv_acc)

    lane = lax.broadcasted_iota(jnp.int32, (1, PAIR), 1)

    def prepare_q(slot):
        q = qbuf[slot, :, 0:ROWS, :].reshape(CHUNK, PAIR).astype(F32)
        g = qbuf[slot, :, ROWS : 2 * ROWS, :].reshape(CHUNK, PAIR).astype(F32)
        for h in range(2):
            own = jnp.where(lane // HEAD == h, 1.0, 0.0).astype(F32)
            qm[slot, h] = (q * (own * HEAD**-0.5)).astype(BF)
            gm[slot, h] = (g * own).astype(BF)
        for i in range(GROUP // 2):
            part = qbuf[slot, 2 * i, 2 * ROWS : SIDE, :].astype(F32)
            part += qbuf[slot, 2 * i + 1, 2 * ROWS : SIDE, :].astype(F32)
            terms[slot, 0:4, i * PAIR : (i + 1) * PAIR] = part[0:4] + part[4:8] + part[8:12]

    def prepare_k(slot):
        k = kbuf[slot, :, 0:ROWS, :].reshape(CHUNK, PAIR).astype(F32)
        kt[slot] = (k * HEAD**-0.5).T.astype(BF)

    for d in range(1, GROUP):
        in_copy(1, d).wait_recv()
    ring_copy(1, 1).start()
    ring_copy(1, -1).start()
    for d in range(1, GROUP):
        in_copy(0, d).wait_recv()
    ring_copy(0, 1).start()
    ring_copy(0, -1).start()
    prepare_k(0)
    prepare_q(0)

    def tile(kslot, qslot):
        k = kbuf[kslot, :, 0:ROWS, :].reshape(CHUNK, PAIR)
        v = kbuf[kslot, :, ROWS : 2 * ROWS, :].reshape(CHUNK, PAIR)
        for h in range(2):
            q = qm[qslot, h]
            g = gm[qslot, h]
            probs = jnp.exp(dot_nt(k, q) - terms[qslot, h : h + 1, :])
            grad = probs * (dot_nt(v, g) - terms[qslot, 2 + h : 3 + h, :])
            grad = grad.astype(BF)
            dv_acc[kslot] += dot_nn(probs.astype(BF), g)
            dk_acc[kslot] += dot_nn(grad, q)
            rows = slice(h * HEAD, (h + 1) * HEAD)
            dq_acc[qslot, rows, :] += dot_nn(kt[kslot, rows, :], grad)

    def send_kv(slot):
        kv_send[slot - 1, 0] = dk_acc[slot].astype(BF)
        kv_send[slot - 1, 1] = dv_acc[slot].astype(BF)
        kv_copy(slot).start()

    def send_q(slot):
        q_send[slot - 1] = dq_acc[slot].T.astype(BF)
        q_copy(slot).start()

    def step(t, carry):
        turn = (t + 3) // 4
        last = t // 13
        kslot = (turn + (turn // 2) * (1 - turn // 4) - 2 * (turn // 3) * (1 - turn // 4)) % 4
        place = ((t + 3) % 4) * ((t + 15) // 16)
        qslot = (1 - last) * place + last * ((place + 2) % 3 + 1)

        @pl.when(t == 1)
        def _():
            ring_copy(1, -1).wait_recv()
            forward_copy(1, 0).start()
            ring_copy(1, 1).wait_recv()
            forward_copy(1, 1).start()
            ring_copy(0, -1).wait_recv()
            forward_copy(0, 0).start()
            ring_copy(0, 1).wait_recv()
            forward_copy(0, 1).start()
            prepare_k(1)
            prepare_k(2)
            prepare_q(1)
            prepare_q(2)

        @pl.when(t == 4)
        def _():
            forward_copy(0, 0).wait_recv()
            forward_copy(0, 1).wait_recv()
            prepare_q(3)

        @pl.when(t == 5)
        def _():
            forward_copy(1, 0).wait_recv()
            forward_copy(1, 1).wait_recv()
            prepare_k(3)
            send_kv(1)

        @pl.when(t == 9)
        def _():
            send_kv(3)

        @pl.when(t == 13)
        def _():
            send_kv(2)

        @pl.when(t == 14)
        def _():
            send_q(3)

        @pl.when(t == 15)
        def _():
            send_q(1)

        tile(kslot, qslot)
        return carry

    lax.fori_loop(0, STEPS, step, 0)
    send_q(2)

    for slot in (1, 3, 2):
        kv_copy(slot).wait_recv()
    for i, acc in enumerate((dk_acc, dv_acc)):
        total = acc[0]
        for slot in (1, 2, 3):
            total = total + kv_recv[slot - 1, i].astype(F32)
        acc[0] = total
        for d in range(1, GROUP):
            back_kv[d, i] = total[d * ROWS : (d + 1) * ROWS].astype(BF)
    for d in (4, 5, 3, 2, 6, 7, 1):
        out_copy(1, d).start()
    for slot in (3, 1, 2):
        q_copy(slot).wait_recv()
    total = dq_acc[0].T
    for slot in (1, 2, 3):
        total = total + q_recv[slot - 1].astype(F32)
    for d in range(1, GROUP):
        back_q[d] = total[d * ROWS : (d + 1) * ROWS].astype(BF)
    for d in (4, 5, 3, 2, 6, 7, 1):
        out_copy(0, d).start()

    def columns(d):
        return pl.ds(pl.multiple_of(lax.rem(me + d, GROUP) * PAIR, PAIR), PAIR)

    dk_out[:, columns(0)] = dk_acc[0, 0:ROWS]
    dv_out[:, columns(0)] = dv_acc[0, 0:ROWS]
    dq_out[:, columns(0)] = total[0:ROWS]
    for d in range(1, GROUP):
        out_copy(1, d).wait_recv()
        dk_out[:, columns(d)] = home_kv[d, 0].astype(F32)
        dv_out[:, columns(d)] = home_kv[d, 1].astype(F32)
    for d in range(1, GROUP):
        out_copy(0, d).wait_recv()
        dq_out[:, columns(d)] = home_q[d].astype(F32)

    for side in range(2):
        for d in range(1, GROUP):
            in_copy(side, d).wait_send()
            out_copy(side, d).wait_send()
        ring_copy(side, 1).wait_send()
        ring_copy(side, -1).wait_send()
        forward_copy(side, 0).wait_send()
        forward_copy(side, 1).wait_send()
    for slot in (1, 2, 3):
        kv_copy(slot).wait_send()
        q_copy(slot).wait_send()


def shards(queries, key_rows, value_rows, output_rows, grad_out, log_sums):
    vmem = pl.BlockSpec(memory_space=pltpu.VMEM)
    out = jax.ShapeDtypeStruct((ROWS, GROUP * PAIR), F32)
    dma = pltpu.SemaphoreType.DMA
    return pl.pallas_call(
        kernel,
        out_shape=(out, out, out),
        in_specs=[vmem] * 6,
        out_specs=(vmem, vmem, vmem),
        scratch_shapes=[
            pltpu.VMEM((GROUP, SIDE, PAIR), BF),
            pltpu.VMEM((GROUP, 2 * ROWS, PAIR), BF),
            pltpu.VMEM((RING, GROUP, SIDE, PAIR), BF),
            pltpu.VMEM((RING, GROUP, 2 * ROWS, PAIR), BF),
            pltpu.VMEM((RING, 2, CHUNK, PAIR), BF),
            pltpu.VMEM((RING, 2, CHUNK, PAIR), BF),
            pltpu.VMEM((RING, PAIR, CHUNK), BF),
            pltpu.VMEM((RING, 8, CHUNK), F32),
            pltpu.VMEM((RING, PAIR, CHUNK), F32),
            pltpu.VMEM((RING, CHUNK, PAIR), F32),
            pltpu.VMEM((RING, CHUNK, PAIR), F32),
            pltpu.VMEM((3, 2, CHUNK, PAIR), BF),
            pltpu.VMEM((3, 2, CHUNK, PAIR), BF),
            pltpu.VMEM((3, CHUNK, PAIR), BF),
            pltpu.VMEM((3, CHUNK, PAIR), BF),
            pltpu.VMEM((GROUP, 2, ROWS, PAIR), BF),
            pltpu.VMEM((GROUP, ROWS, PAIR), BF),
            pltpu.VMEM((GROUP, 2, ROWS, PAIR), BF),
            pltpu.VMEM((GROUP, ROWS, PAIR), BF),
            dma((2, GROUP)), dma((2, GROUP)),
            dma((2, 4)), dma((2, 4)),
            dma((2, 4)), dma((2, 4)),
            dma((2, GROUP)), dma((2, GROUP)),
        ],
        compiler_params=pltpu.CompilerParams(
            collective_id=0, has_side_effects=True, vmem_limit_bytes=48 * 2**20
        ),
        cost_estimate=pl.CostEstimate(
            flops=5 * 2**30, bytes_accessed=2**21, transcendentals=2**23
        ),
    )(queries, key_rows, value_rows, output_rows, grad_out, log_sums)


def solution(mesh):
    q_side = P(("pb", "ka"), None)
    k_side = P(("ka", "pb"), None)
    return jax.shard_map(
        shards,
        mesh=mesh,
        in_specs=(q_side, k_side, k_side, q_side, q_side, q_side),
        out_specs=(q_side, k_side, k_side),
        check_vma=False,
    )
```

time: 532 us -> 64.6 us (0.12)
  waiting for transfers between devices: 278 us -> 0 us
  local copies, waits for them, and re-layouts: 136 us -> 7.41 us
  matrix products: 73.2 us -> 0 us
  Pallas kernels: 0 us -> 56.3 us
  blocking collectives: 22.1 us -> 0 us
  between operations: 14.7 us -> 0.64 us
    all_gather x5 -> x0, waiting for transfers between devices: 143 us -> none  [the longest x1 46.9 us: shards(): lax.all_gather(value_rows, 'pb', axis=0, tiled=True)]
    reduce_scatter x3 -> x0, waiting for transfers between devices: 132 us -> none  [the longest x1 66.6 us: shards(): lax.psum_scatter(key_partial, 'pb', scatter_dimension=0, tiled=True)]
    dot_general x40 -> x0, matrix products: 73.2 us -> none  [the longest x8 21.7 us: group_terms(): jnp.einsum('qhd,khd->hqk', grad_group, value_group, preferred_element_typ...]
    pallas_call x0 -> x1, Pallas kernels: none -> 56.3 us  [shards(): pl.pallas_call(kernel, out_shape=(out, out, out), in_specs=[vmem] * 6, ou...]
    unnamed x130 -> x14, local copies, waits for them, and re-layouts: 48.4 us -> 7.41 us
    reshape x24 -> x0, local copies, waits for them, and re-layouts: 40 us -> none  [the longest x8 14.3 us: key_side_terms(): grad_values.reshape(key_count, -1)]
    slice x36 -> x0, local copies, waits for them, and re-layouts: 36.6 us -> none  [the longest x9 16.6 us: group_terms(): grad_block[:, first:last].reshape(grad_block.shape[0], per_group, head_size)]
    all_gather x1 -> x0, blocking collectives: 22.1 us -> none  [shards(): sums_rows = lax.all_gather(log_sums, 'ka', axis=0, tiled=True)]
  transfers between devices with their start and end apart: 8 -> 0, of which waited for: 7 -> 0; matrix products, arithmetic and copies ran while one was open for 23% -> 0% of each run, Pallas kernels for 0% -> 0%
where the time goes in v1:
time: 64.6 us; the launch traced here: 64.4 us
  Pallas kernels  56.3 us (87%)
  local copies, waits for them, and re-layouts  7.41 us (11%)
    pallas_call x1, Pallas kernels, shards(): pl.pallas_call(kernel, out_shape=(out, out, out), in_specs=[vmem] * 6, ou...  56.3 us
    unnamed x14, local copies, waits for them, and re-layouts  7.41 us

profile of v1, /device:TPU:1, one launch (start us, length us, event | category | flops | bytes accessed | tf_op | source)
XLA Modules:
  0.0 64.4 jit_solution(37282525170019405)
XLA Ops:
  0.6 0.8 %copy.9.sums_in = f32[64,16]{1,0:T(8,128)S(1)} copy(f32[64,16]{0,1:T(8,128)} %param.11) | data formatting | bytes 8192 | tf_op args[5]
  1.4 0.0 copy-start
  1.4 0.9 %copy-done = bf16[64,1024]{1,0:T(8,128)(2,1)S(1)} copy-done((bf16[64,1024]{1,0:T(8,128)(2,1)S(1)}, bf16[64,1024]{1,0:T(8,128)(2,1)}, u32[]{:S(2)}) %copy-start) | copy-done | bytes 131096
  2.3 0.0 copy-start.1
  2.3 0.9 %copy-done.1 = bf16[64,1024]{1,0:T(8,128)(2,1)S(1)} copy-done((bf16[64,1024]{1,0:T(8,128)(2,1)S(1)}, bf16[64,1024]{1,0:T(8,128)(2,1)}, u32[]{:S(2)}) %copy-start.1) | copy-done | bytes 131096
  3.2 0.0 copy-start.2
  3.2 0.9 %copy-done.2 = bf16[64,1024]{1,0:T(8,128)(2,1)S(1)} copy-done((bf16[64,1024]{1,0:T(8,128)(2,1)S(1)}, bf16[64,1024]{1,0:T(8,128)(2,1)}, u32[]{:S(2)}) %copy-start.2) | copy-done | bytes 131096
  4.1 0.0 copy-start.3
  4.1 0.9 %copy-done.3 = bf16[64,1024]{1,0:T(8,128)(2,1)S(1)} copy-done((bf16[64,1024]{1,0:T(8,128)(2,1)S(1)}, bf16[64,1024]{1,0:T(8,128)(2,1)}, u32[]{:S(2)}) %copy-start.3) | copy-done | bytes 131096
  5.0 0.0 copy-start.4
  5.0 0.9 %copy-done.4 = bf16[64,1024]{1,0:T(8,128)(2,1)S(1)} copy-done((bf16[64,1024]{1,0:T(8,128)(2,1)S(1)}, bf16[64,1024]{1,0:T(8,128)(2,1)}, u32[]{:S(2)}) %copy-start.4) | copy-done | bytes 131096
  5.9 56.3 %shard_map.85 = (f32[64,1024]{1,0:T(8,128)S(1)}, f32[64,1024]{1,0:T(8,128)S(1)}, f32[64,1024]{1,0:T(8,128)S(1)}) custom-call(bf16[64,1024]{1,0:T(8,128)(2,1)S(1)} %copy-done, bf16[64,1024]{1,0:T(8,128)(2,1)S(1)} %copy-done.1, bf16[64,1024]{1,0:T(8,128)(2,1)S(1)} %copy-done.2, bf16[64,1024]{1,0:T(8,128)(2,1)S(1)} %copy-done.3, ...), custom_call_target="tpu_custom_call" | custom-call | flops 5368709120 | bytes 2097152 | tf_op jit(solution)/shard_map/pallas_call | solution.py:337
  62.3 0.7 %copy.13 = f32[64,1024]{1,0:T(8,128)} copy(f32[64,1024]{1,0:T(8,128)S(1)} %get-tuple-element.6) | data formatting | bytes 524288
  63.0 0.7 %copy.14 = f32[64,1024]{1,0:T(8,128)} copy(f32[64,1024]{1,0:T(8,128)S(1)} %get-tuple-element.7) | data formatting | bytes 524288
  63.7 0.7 %copy.15 = f32[64,1024]{1,0:T(8,128)} copy(f32[64,1024]{1,0:T(8,128)S(1)} %get-tuple-element.8) | data formatting | bytes 524288
Async XLA Ops:
  1.4 0.9 %copy-start = (bf16[64,1024]{1,0:T(8,128)(2,1)S(1)}, bf16[64,1024]{1,0:T(8,128)(2,1)}, u32[]{:S(2)}) copy-start(bf16[64,1024]{1,0:T(8,128)(2,1)} %q_in.1) | copy-start | bytes 393220
  2.3 0.9 %copy-start.1 = (bf16[64,1024]{1,0:T(8,128)(2,1)S(1)}, bf16[64,1024]{1,0:T(8,128)(2,1)}, u32[]{:S(2)}) copy-start(bf16[64,1024]{1,0:T(8,128)(2,1)} %k_in.1) | copy-start | bytes 393220
  3.2 0.9 %copy-start.2 = (bf16[64,1024]{1,0:T(8,128)(2,1)S(1)}, bf16[64,1024]{1,0:T(8,128)(2,1)}, u32[]{:S(2)}) copy-start(bf16[64,1024]{1,0:T(8,128)(2,1)} %v_in.1) | copy-start | bytes 393220
  4.1 0.9 %copy-start.3 = (bf16[64,1024]{1,0:T(8,128)(2,1)S(1)}, bf16[64,1024]{1,0:T(8,128)(2,1)}, u32[]{:S(2)}) copy-start(bf16[64,1024]{1,0:T(8,128)(2,1)} %o_in.1) | copy-start | bytes 393220
  5.0 0.9 %copy-start.4 = (bf16[64,1024]{1,0:T(8,128)(2,1)S(1)}, bf16[64,1024]{1,0:T(8,128)(2,1)}, u32[]{:S(2)}) copy-start(bf16[64,1024]{1,0:T(8,128)(2,1)} %g_in.1) | copy-start | bytes 393220

commit v2 on v1

v2 whole, which is shorter than its diff:
```python
import functools

import jax
import jax.numpy as jnp
from jax import lax
from jax.experimental import pallas as pl
from jax.experimental.pallas import tpu as pltpu
from jax.sharding import PartitionSpec as P

BF = jnp.bfloat16
F32 = jnp.float32
MESH = pl.DeviceIdType.MESH

ROWS = 64
PAIR = 128
HEAD = 64
GROUP = 8
RING = 4
CHUNK = 2 * RING * ROWS
SIDE = 2 * ROWS + 16
OFFSETS = (0, 1, -1, 2)
SLOT_AT = {1: 2, -1: 1, 2: 3}
FAR = (1, 2, 3)
STEPS = RING * RING
TILES = (
    (0, 0), (1, 0), (0, 1), (1, 1), (2, 0), (2, 1), (2, 2), (1, 2),
    (1, 3), (2, 3), (3, 1), (3, 2), (3, 3), (3, 0), (0, 2), (0, 3),
)
FORWARD_LAST = 3
HOP_AFTER = 4


def dot_nn(a, b):
    return jnp.dot(a, b, preferred_element_type=F32)


def dot_nt(a, b):
    return lax.dot_general(a, b, (((1,), (1,)), ((), ())), preferred_element_type=F32)


def split3(value):
    high = value.astype(BF)
    rest = value - high.astype(F32)
    mid = rest.astype(BF)
    low = (rest - mid.astype(F32)).astype(BF)
    return high, mid, low


def select_rows(dot, matrix, value):
    high, mid, low = split3(value)
    return dot(matrix, high) + dot(matrix, mid) + dot(matrix, low)


def kernel(
    q_hbm, k_hbm, v_hbm, o_hbm, g_hbm, sums_hbm,
    out_ref,
    q_in, k_in, v_in, o_in, g_in, sums_in, load_sem,
    stage_q, stage_k, qbuf, kbuf, qm, gm, kt, terms,
    dq_acc, dk_acc, dv_acc,
    ring_kv, ring_q, came_kv, came_q, back_kv, back_q, home_kv, home_q,
    near_kv, near_q, direct_kv, direct_q,
    near_sem, cross_sem, ring_sem, sum_sem, back_sem, direct_sem,
):
    loads = [
        pltpu.make_async_copy(src, dst, load_sem.at[i])
        for i, (src, dst) in enumerate((
            (k_hbm, k_in), (v_hbm, v_in), (g_hbm, g_in), (o_hbm, o_in), (sums_hbm, sums_in),
            (q_hbm, q_in),
        ))
    ]
    for load in loads:
        load.start()

    pb = lax.axis_index("pb")
    ka = lax.axis_index("ka")
    y = lax.rem(pb, 4)
    z_hi = pb // 4
    me = lax.rem(ka, 8)
    z_lo = ka // 8
    z = z_hi * 2 + z_lo

    x = me // 2
    core = lax.rem(me, 2)

    pairs = {
        (offset, other): lax.rem(x + (offset + 4), 4) * 2 + (1 - core if other else core)
        for offset in OFFSETS
        for other in (0, 1)
    }
    places = {}
    for offset in OFFSETS:
        at_y = lax.rem(y + (offset + 4), 4)
        at_z = lax.rem(z + (offset + 4), 4)
        for other in (0, 1):
            mine = z_lo * 8 + pairs[0, other]
            places["x", offset, other] = (pb, z_lo * 8 + pairs[offset, other])
            places["y", offset, other] = (z_hi * 4 + at_y, mine)
            places["z", offset, other] = (
                (at_z // 2) * 4 + y, lax.rem(at_z, 2) * 8 + pairs[0, other]
            )

    def pair_at(offset, other):
        return pairs[2 if offset == -2 else offset, other]

    def along_x(offset, other):
        return places["x", offset, other]

    def along_y(offset, other=0):
        return places["y", offset, other]

    def along_z(offset, other=0):
        return places["z", offset, other]

    rings = (along_y, along_z)

    barrier = pltpu.get_barrier_semaphore()
    for peer in [along_x(0, 1)] + [
        along(offset, other)
        for along in (along_x, along_y, along_z)
        for offset in OFFSETS[1:]
        for other in (0, 1)
    ]:
        pl.semaphore_signal(barrier, inc=1, device_id=peer, device_id_type=MESH)

    def remote(src, dst, sem, index, peer):
        return pltpu.make_async_remote_copy(
            src_ref=src, dst_ref=dst, send_sem=sem.at[(0, *index)], recv_sem=sem.at[(1, *index)],
            device_id=peer, device_id_type=MESH,
        )

    stages, bufs = (stage_q, stage_k), (qbuf, kbuf)
    backs, homes = (back_q, back_kv), (home_q, home_kv)
    partials, cames = (ring_q, ring_kv), (came_q, came_kv)
    nears, directs = (near_q, near_kv), (direct_q, direct_kv)
    others = slice(1, 8)
    afar = slice(2, 8)

    def near_copy(side, offset, other):
        piece = 2 * SLOT_AT.get(offset, 0) + other
        return remote(
            stages[side].at[pair_at(0, other)], bufs[side].at[0, piece],
            near_sem, (side,), rings[side](offset, other),
        )

    def near_all(side):
        view = bufs[side].at[0, others]
        return remote(view, view, near_sem, (side,), along_x(0, 1))

    def cross_copy(side, offset, other):
        chunk = SLOT_AT[offset]
        return remote(
            stages[side].at[pair_at(offset, other)], bufs[side].at[chunk, other],
            cross_sem, (side, chunk), along_x(offset, other),
        )

    def cross_all(side, chunk):
        view = bufs[side].at[chunk, 0:2]
        return remote(view, view, cross_sem, (side, chunk), along_x(0, 1))

    def ring_copy(side, chunk, offset):
        first = 2 * SLOT_AT[offset]
        return remote(
            bufs[side].at[chunk, 0:2], bufs[side].at[chunk, first : first + 2],
            ring_sem, (side, chunk), rings[side](offset),
        )

    def ring_all(side, chunk):
        view = bufs[side].at[chunk, afar]
        return remote(view, view, ring_sem, (side, chunk), along_x(0, 1))

    def sum_copy(side, chunk, offset):
        return remote(
            partials[side].at[chunk, OFFSETS.index(offset)],
            cames[side].at[chunk, SLOT_AT[offset]],
            sum_sem, (side, chunk), rings[side](offset),
        )

    def sum_all(side, chunk):
        view = cames[side].at[chunk, 1:4]
        return remote(view, view, sum_sem, (side, chunk), along_x(0, 1))

    def back_copy(side, chunk, other):
        piece = 2 * chunk + other
        return remote(
            backs[side].at[piece], homes[side].at[piece],
            back_sem, (side,), along_x(OFFSETS[chunk], other),
        )

    def back_all(side):
        view = homes[side].at[afar]
        return remote(view, view, back_sem, (side,), along_x(0, 1))

    def direct_copy(side, offset, other):
        return remote(
            nears[side].at[2 * OFFSETS.index(offset) + other],
            directs[side].at[2 * SLOT_AT.get(offset, 0) + other],
            direct_sem, (side,), rings[side](offset, other),
        )

    def direct_all(side):
        view = directs[side].at[others]
        return remote(view, view, direct_sem, (side,), along_x(0, 1))

    near = [(offset, other) for offset in (2, 1, -1, 0) for other in (0, 1)][:-2] + [(0, 1)]

    loads[0].wait()
    loads[1].wait()
    for p in range(GROUP):
        cols = slice(p * PAIR, (p + 1) * PAIR)
        stage_k[p, 0:ROWS] = k_in[:, cols]
        stage_k[p, ROWS : 2 * ROWS] = v_in[:, cols]
    kbuf[0, 0] = stage_k[me]
    for load in loads[2:]:
        load.wait()
    for p in range(GROUP):
        cols = slice(p * PAIR, (p + 1) * PAIR)
        stage_q[p, 0:ROWS] = q_in[:, cols]
        stage_q[p, ROWS : 2 * ROWS] = g_in[:, cols]

    product = g_in[...].astype(F32) * o_in[...].astype(F32)
    product = jnp.concatenate([product, product], axis=0)
    sums = jnp.concatenate([sums_in[...], sums_in[...]], axis=1)
    count = 16 * GROUP

    def row_of(shape):
        return lax.broadcasted_iota(jnp.int32, shape, 0)

    def col_of(shape):
        return lax.broadcasted_iota(jnp.int32, shape, 1)

    def pick(width, first, per_head):
        row, col = row_of((count, width)), col_of((count, width))
        kind = row % 4
        head = 2 * (row // 16) + kind - first
        hit = (row % 16 < 12) & (kind >= first) & (kind < first + 2) & (col // per_head == head)
        return jnp.where(hit, 1.0, 0.0).astype(BF)

    value = select_rows(dot_nt, pick(GROUP * PAIR, 2, HEAD), product)
    value += select_rows(dot_nn, pick(16, 0, 1), sums)
    high = value.astype(BF).astype(F32)
    mid = (value - high).astype(BF).astype(F32)
    low = value - high - mid
    row, col = row_of((count, PAIR)), col_of((count, PAIR))
    third = (row % 16) // 4
    value = jnp.where(third == 0, high, jnp.where(third == 1, mid, low))
    value = jnp.where(col // ROWS == (row // 16 + me) % 2, value, 0.0).astype(BF)
    for p in range(GROUP):
        stage_q[p, 2 * ROWS : SIDE] = value[16 * p : 16 * (p + 1)]

    qbuf[0, 0] = stage_q[me]

    pl.semaphore_wait(barrier, 19)
    for offset, other in near:
        near_copy(1, offset, other).start()
        near_copy(0, offset, other).start()
    for offset in (1, -1):
        for other in (0, 1):
            cross_copy(1, offset, other).start()
            cross_copy(0, offset, other).start()
    dq_acc[...] = jnp.zeros_like(dq_acc)
    dk_acc[...] = jnp.zeros_like(dk_acc)
    dv_acc[...] = jnp.zeros_like(dv_acc)

    lane = lax.broadcasted_iota(jnp.int32, (1, PAIR), 1)

    def prepare_q(slot):
        q = qbuf[slot, :, 0:ROWS, :].reshape(CHUNK, PAIR)
        g = qbuf[slot, :, ROWS : 2 * ROWS, :].reshape(CHUNK, PAIR)
        for h in range(2):
            own = jnp.where(lane // HEAD == h, 1.0, 0.0)
            qm[slot, h] = q * (own * HEAD**-0.5).astype(BF)
            gm[slot, h] = g * own.astype(BF)
        for i in range(RING):
            part = qbuf[slot, 2 * i, 2 * ROWS : SIDE, :].astype(F32)
            part += qbuf[slot, 2 * i + 1, 2 * ROWS : SIDE, :].astype(F32)
            terms[slot, 0:4, i * PAIR : (i + 1) * PAIR] = part[0:4] + part[4:8] + part[8:12]

    def prepare_k(slot):
        k = kbuf[slot, :, 0:ROWS, :].reshape(CHUNK, PAIR).astype(F32)
        kt[slot] = (k * HEAD**-0.5).T.astype(BF)

    def pass_on(chunk):
        for side in (1, 0):
            cross_all(side, chunk).wait_recv()
            for offset in OFFSETS[1:]:
                ring_copy(side, chunk, offset).start()

    def arrive(side, chunk):
        (near_all(side) if chunk == 0 else ring_all(side, chunk)).wait_recv()
        (prepare_q, prepare_k)[side](chunk)

    pass_on(1)
    pass_on(2)
    for other in (0, 1):
        cross_copy(1, 2, other).start()
        cross_copy(0, 2, other).start()
    arrive(1, 0)
    arrive(0, 0)

    def tile(kslot, qslot):
        k = kbuf[kslot, :, 0:ROWS, :].reshape(CHUNK, PAIR)
        v = kbuf[kslot, :, ROWS : 2 * ROWS, :].reshape(CHUNK, PAIR)
        for h in range(2):
            q = qm[qslot, h]
            g = gm[qslot, h]
            probs = jnp.exp(dot_nt(k, q) - terms[qslot, h : h + 1, :])
            grad = probs * (dot_nt(v, g) - terms[qslot, 2 + h : 3 + h, :])
            grad = grad.astype(BF)
            dv_acc[kslot] += dot_nn(probs.astype(BF), g)
            dk_acc[kslot] += dot_nn(grad, q)
            rows = slice(h * HEAD, (h + 1) * HEAD)
            dq_acc[qslot, rows, :] += dot_nn(kt[kslot, rows, :], grad)

    half = 2 * ROWS

    def send_sums(side, chunk):
        if side:
            for slot in FAR:
                rows = slice(slot * half, (slot + 1) * half)
                ring_kv[chunk, slot, 0] = dk_acc[chunk, rows].astype(BF)
                ring_kv[chunk, slot, 1] = dv_acc[chunk, rows].astype(BF)
        else:
            for slot in FAR:
                rows = slice(slot * half, (slot + 1) * half)
                ring_q[chunk, slot] = dq_acc[chunk, :, rows].T.astype(BF)
        for offset in OFFSETS[1:]:
            sum_copy(side, chunk, offset).start()

    def hop(side, chunk):
        sum_all(side, chunk).wait_recv()
        if side:
            for i, acc in enumerate((dk_acc, dv_acc)):
                total = acc[chunk, 0:half]
                for slot in FAR:
                    total = total + came_kv[chunk, slot, i].astype(F32)
                for other in (0, 1):
                    rows = slice(other * ROWS, (other + 1) * ROWS)
                    back_kv[2 * chunk + other, i] = total[rows].astype(BF)
        else:
            total = dq_acc[chunk, :, 0:half].T
            for slot in FAR:
                total = total + came_q[chunk, slot].astype(F32)
            for other in (0, 1):
                back_q[2 * chunk + other] = total[other * ROWS : (other + 1) * ROWS].astype(BF)
        for other in (0, 1):
            back_copy(side, chunk, other).start()

    def send_direct(side):
        for slot in range(RING):
            for other in (0, 1):
                first = slot * half + other * ROWS
                rows = slice(first, first + ROWS)
                if side:
                    near_kv[2 * slot + other, 0] = dk_acc[0, rows].astype(BF)
                    near_kv[2 * slot + other, 1] = dv_acc[0, rows].astype(BF)
            if not side:
                total = dq_acc[0, :, slot * half : (slot + 1) * half].T.astype(BF)
                near_q[2 * slot] = total[0:ROWS]
                near_q[2 * slot + 1] = total[ROWS:half]
        for offset, other in near:
            direct_copy(side, offset, other).start()

    events = {FORWARD_LAST: [(pass_on, (3,))]}
    seen = {(0, 0), (1, 0)}
    left = {(side, chunk): RING for side in range(2) for chunk in range(RING)}
    for i, order in enumerate(TILES):
        for side in (1, 0):
            chunk = order[1 - side]
            if (side, chunk) not in seen:
                seen.add((side, chunk))
                events.setdefault(i, []).append((arrive, (side, chunk)))
            left[side, chunk] -= 1
            if not left[side, chunk]:
                if chunk:
                    events.setdefault(i + 1, []).append((send_sums, (side, chunk)))
                    after = min(i + 1 + HOP_AFTER, STEPS + 1)
                    events.setdefault(after, []).append((hop, (side, chunk)))
                else:
                    events.setdefault(i + 1, []).append((send_direct, (side,)))

    def run(i):
        for act, operands in events.get(i, []):
            act(*operands)

    def step(t, carry):
        kslot = sum(jnp.where(t == i, order[0], 0) for i, order in enumerate(TILES))
        qslot = sum(jnp.where(t == i, order[1], 0) for i, order in enumerate(TILES))
        for i in sorted(events):
            if i < STEPS:
                pl.when(t == i)(functools.partial(run, i))
        tile(kslot, qslot)
        return carry

    lax.fori_loop(0, STEPS, step, 0)
    run(STEPS)
    run(STEPS + 1)

    def columns(offset, other):
        return pl.ds(pl.multiple_of(pair_at(offset, other) * PAIR, PAIR), PAIR)

    for side in (1, 0):
        back_all(side).wait_recv()
    for chunk in FAR:
        for other in (0, 1):
            cols = columns(-OFFSETS[chunk], other)
            piece = 2 * chunk + other
            out_ref[1, :, cols] = home_kv[piece, 0]
            out_ref[2, :, cols] = home_kv[piece, 1]
            out_ref[0, :, cols] = home_q[piece]
    for side in (0, 1):
        direct_all(side).wait_recv()

    def own_sum(first, parts):
        for part in parts:
            first = first + part.astype(F32)
        return first.astype(BF)

    cols = columns(0, 0)
    out_ref[0, :, cols] = own_sum(
        dq_acc[0, :, 0:half].T[0:ROWS], [direct_q[2 * slot] for slot in FAR]
    )
    for i, acc in enumerate((dk_acc, dv_acc)):
        out_ref[1 + i, :, cols] = own_sum(
            acc[0, 0:ROWS], [direct_kv[2 * slot, i] for slot in FAR]
        )
    cols = columns(0, 1)
    out_ref[0, :, cols] = own_sum(
        direct_q[1].astype(F32), [direct_q[2 * slot + 1] for slot in FAR]
    )
    for i in range(2):
        out_ref[1 + i, :, cols] = own_sum(
            direct_kv[1, i].astype(F32), [direct_kv[2 * slot + 1, i] for slot in FAR]
        )

    for side in range(2):
        near_all(side).wait_send()
        back_all(side).wait_send()
        direct_all(side).wait_send()
        for chunk in FAR:
            cross_all(side, chunk).wait_send()
            ring_all(side, chunk).wait_send()
            sum_all(side, chunk).wait_send()


def shards(queries, key_rows, value_rows, output_rows, grad_out, log_sums):
    vmem = pl.BlockSpec(memory_space=pltpu.VMEM)
    hbm = pl.BlockSpec(memory_space=pltpu.HBM)
    out = jax.ShapeDtypeStruct((ROWS, GROUP * PAIR), F32)
    dma = pltpu.SemaphoreType.DMA
    r = pl.pallas_call(
        kernel,
        out_shape=jax.ShapeDtypeStruct((3, ROWS, GROUP * PAIR), BF),
        in_specs=[hbm] * 6,
        out_specs=vmem,
        scratch_shapes=[pltpu.VMEM((ROWS, GROUP * PAIR), BF)] * 5 + [
            pltpu.VMEM((2 * GROUP, ROWS), F32),
            dma((6,)),
            pltpu.VMEM((GROUP, SIDE, PAIR), BF),
            pltpu.VMEM((GROUP, 2 * ROWS, PAIR), BF),
            pltpu.VMEM((RING, GROUP, SIDE, PAIR), BF),
            pltpu.VMEM((RING, GROUP, 2 * ROWS, PAIR), BF),
            pltpu.VMEM((RING, 2, CHUNK, PAIR), BF),
            pltpu.VMEM((RING, 2, CHUNK, PAIR), BF),
            pltpu.VMEM((RING, PAIR, CHUNK), BF),
            pltpu.VMEM((RING, 8, CHUNK), F32),
            pltpu.VMEM((RING, PAIR, CHUNK), F32),
            pltpu.VMEM((RING, CHUNK, PAIR), F32),
            pltpu.VMEM((RING, CHUNK, PAIR), F32),
            pltpu.VMEM((RING, RING, 2, 2 * ROWS, PAIR), BF),
            pltpu.VMEM((RING, RING, 2 * ROWS, PAIR), BF),
            pltpu.VMEM((RING, RING, 2, 2 * ROWS, PAIR), BF),
            pltpu.VMEM((RING, RING, 2 * ROWS, PAIR), BF),
            pltpu.VMEM((GROUP, 2, ROWS, PAIR), BF),
            pltpu.VMEM((GROUP, ROWS, PAIR), BF),
            pltpu.VMEM((GROUP, 2, ROWS, PAIR), BF),
            pltpu.VMEM((GROUP, ROWS, PAIR), BF),
            pltpu.VMEM((GROUP, 2, ROWS, PAIR), BF),
            pltpu.VMEM((GROUP, ROWS, PAIR), BF),
            pltpu.VMEM((GROUP, 2, ROWS, PAIR), BF),
            pltpu.VMEM((GROUP, ROWS, PAIR), BF),
            dma((2, 2)),
            dma((2, 2, RING)),
            dma((2, 2, RING)),
            dma((2, 2, RING)),
            dma((2, 2)),
            dma((2, 2)),
        ],
        compiler_params=pltpu.CompilerParams(
            collective_id=0, has_side_effects=True, vmem_limit_bytes=56 * 2**20
        ),
        cost_estimate=pl.CostEstimate(
            flops=5 * 2**30, bytes_accessed=2**21, transcendentals=2**23
        ),
    )(queries, key_rows, value_rows, output_rows, grad_out, log_sums.T)
    return r[0].astype(F32), r[1].astype(F32), r[2].astype(F32)


def solution(mesh):
    q_side = P(("pb", "ka"), None)
    k_side = P(("ka", "pb"), None)
    return jax.shard_map(
        shards,
        mesh=mesh,
        in_specs=(q_side, k_side, k_side, q_side, q_side, q_side),
        out_specs=(q_side, k_side, k_side),
        check_vma=False,
    )
```

time: 64.6 us -> 54.9 us (0.85)
  local copies, waits for them, and re-layouts: 7.41 us -> 0 us
  Pallas kernels: 56.3 us -> 52.2 us
  other arithmetic: 0 us -> 1.93 us
    unnamed x14 -> x0, local copies, waits for them, and re-layouts: 7.41 us -> none
    pallas_call x1, Pallas kernels: 56.3 us -> 52.2 us  [shards(): pl.pallas_call(kernel, out_shape=jax.ShapeDtypeStruct((3, ROWS, GROUP * P...]
    convert_element_type x0 -> x1, other arithmetic: none -> 1.93 us  [shards(): return (r[0].astype(F32), r[1].astype(F32), r[2].astype(F32))]
where the time goes in v2:
time: 54.9 us; the launch traced here: 54.7 us
  Pallas kernels  52.2 us (95%)
  other arithmetic  1.93 us (4%)
  between operations  0.64 us (1%)
    pallas_call x1, Pallas kernels, shards(): pl.pallas_call(kernel, out_shape=jax.ShapeDtypeStruct((3, ROWS, GROUP * P...  52.2 us
    convert_element_type x1, other arithmetic, shards(): return (r[0].astype(F32), r[1].astype(F32), r[2].astype(F32))  1.93 us

profile of v2, /device:TPU:1, one launch (start us, length us, event | category | flops | bytes accessed | tf_op | source)
XLA Modules:
  0.0 54.7 jit_solution(12741566192838431104)
XLA Ops:
  0.6 52.2 %shard_map.85 = bf16[3,64,1024]{2,1,0:T(8,128)(2,1)} custom-call(bf16[64,1024]{1,0:T(8,128)(2,1)} %q_hbm.1, bf16[64,1024]{1,0:T(8,128)(2,1)} %k_hbm.1, bf16[64,1024]{1,0:T(8,128)(2,1)} %v_hbm.1, bf16[64,1024]{1,0:T(8,128)(2,1)} %o_hbm.1, bf16[64,1024]{1,0:T(8,128)(2,1)} %g_hbm.1, f32[16,64]{1,0:T(8,128)} %bitcast.10), custom_call_target="tpu_custom_call" | custom-call | flops 5368709120 | bytes 2097152 | tf_op jit(solution)/shard_map/pallas_call | solution.py:450
  52.8 1.9 %bitcast_convert_fusion = (f32[64,1024]{1,0:T(8,128)}, f32[64,1024]{1,0:T(8,128)}, f32[64,1024]{1,0:T(8,128)}) fusion(bf16[3,64,1024]{2,1,0:T(8,128)(2,1)} %shard_map.85), kind=kLoop, calls=%fused_computation | loop fusion | flops 196608 | bytes 1179648 | tf_op jit(solution)/shard_map/convert_element_type | solution.py:495

commit v3 on v2

--- a/solution.py
+++ b/solution.py
@@ -23,11 +23,11 @@
 FAR = (1, 2, 3)
 STEPS = RING * RING
 TILES = (
-    (0, 0), (1, 0), (0, 1), (1, 1), (2, 0), (2, 1), (2, 2), (1, 2),
-    (1, 3), (2, 3), (3, 1), (3, 2), (3, 3), (3, 0), (0, 2), (0, 3),
+    (0, 0), (1, 0), (1, 1), (2, 0), (2, 1), (2, 2), (1, 2), (1, 3),
+    (2, 3), (0, 3), (3, 3), (3, 0), (3, 1), (3, 2), (0, 1), (0, 2),
 )
-FORWARD_LAST = 3
-HOP_AFTER = 4
+FORWARD_AT = {2: 1, 3: 2}
+HOP_AFTER = 5
 
 
 def dot_nn(a, b):
@@ -57,9 +57,8 @@
     q_in, k_in, v_in, o_in, g_in, sums_in, load_sem,
     stage_q, stage_k, qbuf, kbuf, qm, gm, kt, terms,
     dq_acc, dk_acc, dv_acc,
-    ring_kv, ring_q, came_kv, came_q, back_kv, back_q, home_kv, home_q,
-    near_kv, near_q, direct_kv, direct_q,
-    near_sem, cross_sem, ring_sem, sum_sem, back_sem, direct_sem,
+    ring_kv, came_kv, back_kv, home_kv, near_kv, direct_kv, send_q, came_q, own_q,
+    near_sem, cross_sem, ring_sem, sum_sem, back_sem, direct_sem, query_sem,
 ):
     loads = [
         pltpu.make_async_copy(src, dst, load_sem.at[i])
@@ -95,6 +94,10 @@
             mine = z_lo * 8 + pairs[0, other]
             places["x", offset, other] = (pb, z_lo * 8 + pairs[offset, other])
             places["y", offset, other] = (z_hi * 4 + at_y, mine)
+            for chunk in FAR:
+                places["xy", chunk, offset, other] = (
+                    z_hi * 4 + at_y, z_lo * 8 + pairs[OFFSETS[chunk], other]
+                )
             places["z", offset, other] = (
                 (at_z // 2) * 4 + y, lax.rem(at_z, 2) * 8 + pairs[0, other]
             )
@@ -129,9 +132,6 @@
         )
 
     stages, bufs = (stage_q, stage_k), (qbuf, kbuf)
-    backs, homes = (back_q, back_kv), (home_q, home_kv)
-    partials, cames = (ring_q, ring_kv), (came_q, came_kv)
-    nears, directs = (near_q, near_kv), (direct_q, direct_kv)
     others = slice(1, 8)
     afar = slice(2, 8)
 
@@ -168,38 +168,49 @@
         view = bufs[side].at[chunk, afar]
         return remote(view, view, ring_sem, (side, chunk), along_x(0, 1))
 
-    def sum_copy(side, chunk, offset):
-        return remote(
-            partials[side].at[chunk, OFFSETS.index(offset)],
-            cames[side].at[chunk, SLOT_AT[offset]],
-            sum_sem, (side, chunk), rings[side](offset),
-        )
-
-    def sum_all(side, chunk):
-        view = cames[side].at[chunk, 1:4]
-        return remote(view, view, sum_sem, (side, chunk), along_x(0, 1))
-
-    def back_copy(side, chunk, other):
+    def sum_copy(chunk, offset):
+        return remote(
+            ring_kv.at[chunk, OFFSETS.index(offset)], came_kv.at[chunk, SLOT_AT[offset]],
+            sum_sem, (chunk,), along_z(offset),
+        )
+
+    def sum_all(chunk):
+        view = came_kv.at[chunk, 1:4]
+        return remote(view, view, sum_sem, (chunk,), along_x(0, 1))
+
+    def back_copy(chunk, other):
         piece = 2 * chunk + other
         return remote(
-            backs[side].at[piece], homes[side].at[piece],
-            back_sem, (side,), along_x(OFFSETS[chunk], other),
-        )
-
-    def back_all(side):
-        view = homes[side].at[afar]
-        return remote(view, view, back_sem, (side,), along_x(0, 1))
-
-    def direct_copy(side, offset, other):
-        return remote(
-            nears[side].at[2 * OFFSETS.index(offset) + other],
-            directs[side].at[2 * SLOT_AT.get(offset, 0) + other],
-            direct_sem, (side,), rings[side](offset, other),
-        )
-
-    def direct_all(side):
-        view = directs[side].at[others]
-        return remote(view, view, direct_sem, (side,), along_x(0, 1))
+            back_kv.at[piece], home_kv.at[piece],
+            back_sem, (), along_x(OFFSETS[chunk], other),
+        )
+
+    def back_all():
+        view = home_kv.at[afar]
+        return remote(view, view, back_sem, (), along_x(0, 1))
+
+    def direct_copy(offset, other):
+        return remote(
+            near_kv.at[2 * OFFSETS.index(offset) + other],
+            direct_kv.at[2 * SLOT_AT.get(offset, 0) + other],
+            direct_sem, (), along_z(offset, other),
+        )
+
+    def direct_all():
+        view = direct_kv.at[others]
+        return remote(view, view, direct_sem, (), along_x(0, 1))
+
+    def query_copy(chunk, offset, other):
+        peer = places["xy", chunk, offset, other] if chunk else along_y(offset, other)
+        return remote(
+            send_q.at[chunk, 2 * OFFSETS.index(offset) + other],
+            came_q.at[chunk, 2 * SLOT_AT.get(offset, 0) + other],
+            query_sem, (chunk,), peer,
+        )
+
+    def query_all(chunk):
+        view = came_q.at[chunk] if chunk else came_q.at[0, others]
+        return remote(view, view, query_sem, (chunk,), along_x(0, 1))
 
     near = [(offset, other) for offset in (2, 1, -1, 0) for other in (0, 1)][:-2] + [(0, 1)]
 
@@ -290,7 +301,6 @@
         (prepare_q, prepare_k)[side](chunk)
 
     pass_on(1)
-    pass_on(2)
     for other in (0, 1):
         cross_copy(1, 2, other).start()
         cross_copy(0, 2, other).start()
@@ -313,54 +323,45 @@
 
     half = 2 * ROWS
 
-    def send_sums(side, chunk):
-        if side:
+    def send_sums(chunk):
+        for slot in FAR:
+            rows = slice(slot * half, (slot + 1) * half)
+            ring_kv[chunk, slot, 0] = dk_acc[chunk, rows].astype(BF)
+            ring_kv[chunk, slot, 1] = dv_acc[chunk, rows].astype(BF)
+        for offset in OFFSETS[1:]:
+            sum_copy(chunk, offset).start()
+
+    def hop(chunk):
+        sum_all(chunk).wait_recv()
+        for i, acc in enumerate((dk_acc, dv_acc)):
+            total = acc[chunk, 0:half]
             for slot in FAR:
-                rows = slice(slot * half, (slot + 1) * half)
-                ring_kv[chunk, slot, 0] = dk_acc[chunk, rows].astype(BF)
-                ring_kv[chunk, slot, 1] = dv_acc[chunk, rows].astype(BF)
-        else:
-            for slot in FAR:
-                rows = slice(slot * half, (slot + 1) * half)
-                ring_q[chunk, slot] = dq_acc[chunk, :, rows].T.astype(BF)
-        for offset in OFFSETS[1:]:
-            sum_copy(side, chunk, offset).start()
-
-    def hop(side, chunk):
-        sum_all(side, chunk).wait_recv()
-        if side:
-            for i, acc in enumerate((dk_acc, dv_acc)):
-                total = acc[chunk, 0:half]
-                for slot in FAR:
-                    total = total + came_kv[chunk, slot, i].astype(F32)
-                for other in (0, 1):
-                    rows = slice(other * ROWS, (other + 1) * ROWS)
-                    back_kv[2 * chunk + other, i] = total[rows].astype(BF)
-        else:
-            total = dq_acc[chunk, :, 0:half].T
-            for slot in FAR:
-                total = total + came_q[chunk, slot].astype(F32)
+                total = total + came_kv[chunk, slot, i].astype(F32)
             for other in (0, 1):
-                back_q[2 * chunk + other] = total[other * ROWS : (other + 1) * ROWS].astype(BF)
+                rows = slice(other * ROWS, (other + 1) * ROWS)
+                back_kv[2 * chunk + other, i] = total[rows].astype(BF)
         for other in (0, 1):
-            back_copy(side, chunk, other).start()
-
-    def send_direct(side):
-        for slot in range(RING):
-            for other in (0, 1):
-                first = slot * half + other * ROWS
-                rows = slice(first, first + ROWS)
-                if side:
-                    near_kv[2 * slot + other, 0] = dk_acc[0, rows].astype(BF)
-                    near_kv[2 * slot + other, 1] = dv_acc[0, rows].astype(BF)
-            if not side:
-                total = dq_acc[0, :, slot * half : (slot + 1) * half].T.astype(BF)
-                near_q[2 * slot] = total[0:ROWS]
-                near_q[2 * slot + 1] = total[ROWS:half]
+            back_copy(chunk, other).start()
+
+    def send_direct():
+        for piece in range(1, GROUP):
+            rows = slice(piece * ROWS, (piece + 1) * ROWS)
+            near_kv[piece, 0] = dk_acc[0, rows].astype(BF)
+            near_kv[piece, 1] = dv_acc[0, rows].astype(BF)
         for offset, other in near:
-            direct_copy(side, offset, other).start()
-
-    events = {FORWARD_LAST: [(pass_on, (3,))]}
+            direct_copy(offset, other).start()
+
+    def send_query(chunk):
+        total = dq_acc[chunk].T
+        if not chunk:
+            own_q[...] = total[0:ROWS]
+        send_q[chunk] = total.astype(BF).reshape(GROUP, ROWS, PAIR)
+        for offset, other in near + [(0, 0)] * bool(chunk):
+            query_copy(chunk, offset, other).start()
+
+    events = {}
+    for chunk, i in FORWARD_AT.items():
+        events.setdefault(i, []).append((pass_on, (chunk,)))
     seen = {(0, 0), (1, 0)}
     left = {(side, chunk): RING for side in range(2) for chunk in range(RING)}
     for i, order in enumerate(TILES):
@@ -371,12 +372,14 @@
                 events.setdefault(i, []).append((arrive, (side, chunk)))
             left[side, chunk] -= 1
             if not left[side, chunk]:
-                if chunk:
-                    events.setdefault(i + 1, []).append((send_sums, (side, chunk)))
+                if not side:
+                    events.setdefault(i + 1, []).append((send_query, (chunk,)))
+                elif chunk:
+                    events.setdefault(i + 1, []).append((send_sums, (chunk,)))
                     after = min(i + 1 + HOP_AFTER, STEPS + 1)
-                    events.setdefault(after, []).append((hop, (side, chunk)))
+                    events.setdefault(after, []).append((hop, (chunk,)))
                 else:
-                    events.setdefault(i + 1, []).append((send_direct, (side,)))
+                    events.setdefault(i + 1, []).append((send_direct, ()))
 
     def run(i):
         for act, operands in events.get(i, []):
@@ -398,48 +401,42 @@
     def columns(offset, other):
         return pl.ds(pl.multiple_of(pair_at(offset, other) * PAIR, PAIR), PAIR)
 
-    for side in (1, 0):
-        back_all(side).wait_recv()
+    def own_sum(first, parts):
+        for part in parts:
+            first = first + part.astype(F32)
+        return first.astype(BF)
+
+    back_all().wait_recv()
     for chunk in FAR:
         for other in (0, 1):
             cols = columns(-OFFSETS[chunk], other)
             piece = 2 * chunk + other
             out_ref[1, :, cols] = home_kv[piece, 0]
             out_ref[2, :, cols] = home_kv[piece, 1]
-            out_ref[0, :, cols] = home_q[piece]
-    for side in (0, 1):
-        direct_all(side).wait_recv()
-
-    def own_sum(first, parts):
-        for part in parts:
-            first = first + part.astype(F32)
-        return first.astype(BF)
-
-    cols = columns(0, 0)
-    out_ref[0, :, cols] = own_sum(
-        dq_acc[0, :, 0:half].T[0:ROWS], [direct_q[2 * slot] for slot in FAR]
-    )
+    for chunk in range(RING):
+        query_all(chunk).wait_recv()
+        for other in (0, 1):
+            parts = [came_q[chunk, 2 * slot + other] for slot in range(RING)]
+            first = parts[0].astype(F32) if chunk or other else own_q[...]
+            out_ref[0, :, columns(-OFFSETS[chunk], other)] = own_sum(first, parts[1:])
+    direct_all().wait_recv()
     for i, acc in enumerate((dk_acc, dv_acc)):
-        out_ref[1 + i, :, cols] = own_sum(
-            acc[0, 0:ROWS], [direct_kv[2 * slot, i] for slot in FAR]
-        )
-    cols = columns(0, 1)
-    out_ref[0, :, cols] = own_sum(
-        direct_q[1].astype(F32), [direct_q[2 * slot + 1] for slot in FAR]
-    )
-    for i in range(2):
-        out_ref[1 + i, :, cols] = own_sum(
-            direct_kv[1, i].astype(F32), [direct_kv[2 * slot + 1, i] for slot in FAR]
-        )
-
+        for other in (0, 1):
+            parts = [direct_kv[2 * slot + other, i] for slot in range(RING)]
+            first = parts[0].astype(F32) if other else acc[0, 0:ROWS]
+            out_ref[1 + i, :, columns(0, other)] = own_sum(first, parts[1:])
+
+    back_all().wait_send()
+    direct_all().wait_send()
+    for chunk in range(RING):
+        query_all(chunk).wait_send()
+    for chunk in FAR:
+        sum_all(chunk).wait_send()
     for side in range(2):
         near_all(side).wait_send()
-        back_all(side).wait_send()
-        direct_all(side).wait_send()
         for chunk in FAR:
             cross_all(side, chunk).wait_send()
             ring_all(side, chunk).wait_send()
-            sum_all(side, chunk).wait_send()
 
 
 def shards(queries, key_rows, value_rows, output_rows, grad_out, log_sums):
@@ -467,23 +464,21 @@
             pltpu.VMEM((RING, CHUNK, PAIR), F32),
             pltpu.VMEM((RING, CHUNK, PAIR), F32),
             pltpu.VMEM((RING, RING, 2, 2 * ROWS, PAIR), BF),
-            pltpu.VMEM((RING, RING, 2 * ROWS, PAIR), BF),
             pltpu.VMEM((RING, RING, 2, 2 * ROWS, PAIR), BF),
-            pltpu.VMEM((RING, RING, 2 * ROWS, PAIR), BF),
             pltpu.VMEM((GROUP, 2, ROWS, PAIR), BF),
-            pltpu.VMEM((GROUP, ROWS, PAIR), BF),
             pltpu.VMEM((GROUP, 2, ROWS, PAIR), BF),
-            pltpu.VMEM((GROUP, ROWS, PAIR), BF),
             pltpu.VMEM((GROUP, 2, ROWS, PAIR), BF),
-            pltpu.VMEM((GROUP, ROWS, PAIR), BF),
             pltpu.VMEM((GROUP, 2, ROWS, PAIR), BF),
-            pltpu.VMEM((GROUP, ROWS, PAIR), BF),
+            pltpu.VMEM((RING, GROUP, ROWS, PAIR), BF),
+            pltpu.VMEM((RING, GROUP, ROWS, PAIR), BF),
+            pltpu.VMEM((ROWS, PAIR), F32),
             dma((2, 2)),
             dma((2, 2, RING)),
             dma((2, 2, RING)),
-            dma((2, 2, RING)),
-            dma((2, 2)),
-            dma((2, 2)),
+            dma((2, RING)),
+            dma((2,)),
+            dma((2,)),
+            dma((2, RING)),
         ],
         compiler_params=pltpu.CompilerParams(
             collective_id=0, has_side_effects=True, vmem_limit_bytes=56 * 2**20

time: 54.9 us -> 51 us (0.929)
  Pallas kernels: 52.2 us -> 48.3 us
    pallas_call x1, Pallas kernels: 52.2 us -> 48.3 us  [shards(): pl.pallas_call(kernel, out_shape=jax.ShapeDtypeStruct((3, ROWS, GROUP * P...]
where the time goes in v3:
time: 51 us; the launch traced here: 50.9 us
  Pallas kernels  48.3 us (95%)
  other arithmetic  1.93 us (4%)
  between operations  0.64 us (1%)
    pallas_call x1, Pallas kernels, shards(): pl.pallas_call(kernel, out_shape=jax.ShapeDtypeStruct((3, ROWS, GROUP * P...  48.3 us
    convert_element_type x1, other arithmetic, shards(): return (r[0].astype(F32), r[1].astype(F32), r[2].astype(F32))  1.93 us

profile of v3, /device:TPU:1, one launch (start us, length us, event | category | flops | bytes accessed | tf_op | source)
XLA Modules:
  0.0 50.9 jit_solution(15141249270706554500)
XLA Ops:
  0.6 48.3 %shard_map.85 = bf16[3,64,1024]{2,1,0:T(8,128)(2,1)} custom-call(bf16[64,1024]{1,0:T(8,128)(2,1)} %q_hbm.1, bf16[64,1024]{1,0:T(8,128)(2,1)} %k_hbm.1, bf16[64,1024]{1,0:T(8,128)(2,1)} %v_hbm.1, bf16[64,1024]{1,0:T(8,128)(2,1)} %o_hbm.1, bf16[64,1024]{1,0:T(8,128)(2,1)} %g_hbm.1, f32[16,64]{1,0:T(8,128)} %bitcast.10), custom_call_target="tpu_custom_call" | custom-call | flops 5368709120 | bytes 2097152 | tf_op jit(solution)/shard_map/pallas_call | solution.py:447
  48.9 1.9 %bitcast_convert_fusion = (f32[64,1024]{1,0:T(8,128)}, f32[64,1024]{1,0:T(8,128)}, f32[64,1024]{1,0:T(8,128)}) fusion(bf16[3,64,1024]{2,1,0:T(8,128)(2,1)} %shard_map.85), kind=kLoop, calls=%fused_computation | loop fusion | flops 196608 | bytes 1179648 | tf_op jit(solution)/shard_map/convert_element_type | solution.py:490

commit v4 on v3

--- a/solution.py
+++ b/solution.py
@@ -1,5 +1,3 @@
-import functools
-
 import jax
 import jax.numpy as jnp
 from jax import lax
@@ -385,16 +383,9 @@
         for act, operands in events.get(i, []):
             act(*operands)
 
-    def step(t, carry):
-        kslot = sum(jnp.where(t == i, order[0], 0) for i, order in enumerate(TILES))
-        qslot = sum(jnp.where(t == i, order[1], 0) for i, order in enumerate(TILES))
-        for i in sorted(events):
-            if i < STEPS:
-                pl.when(t == i)(functools.partial(run, i))
-        tile(kslot, qslot)
-        return carry
-
-    lax.fori_loop(0, STEPS, step, 0)
+    for i, order in enumerate(TILES):
+        run(i)
+        tile(*order)
     run(STEPS)
     run(STEPS + 1)
 
@@ -444,6 +435,7 @@
     hbm = pl.BlockSpec(memory_space=pltpu.HBM)
     out = jax.ShapeDtypeStruct((ROWS, GROUP * PAIR), F32)
     dma = pltpu.SemaphoreType.DMA
+    arrays = (queries, key_rows, value_rows, output_rows, grad_out, log_sums.T)
     r = pl.pallas_call(
         kernel,
         out_shape=jax.ShapeDtypeStruct((3, ROWS, GROUP * PAIR), BF),
@@ -481,12 +473,12 @@
             dma((2, RING)),
         ],
         compiler_params=pltpu.CompilerParams(
-            collective_id=0, has_side_effects=True, vmem_limit_bytes=56 * 2**20
+            collective_id=0, has_side_effects=True, vmem_limit_bytes=48 * 2**20
         ),
         cost_estimate=pl.CostEstimate(
             flops=5 * 2**30, bytes_accessed=2**21, transcendentals=2**23
         ),
-    )(queries, key_rows, value_rows, output_rows, grad_out, log_sums.T)
+    )(*(pltpu.with_memory_space_constraint(array, pltpu.HBM) for array in arrays))
     return r[0].astype(F32), r[1].astype(F32), r[2].astype(F32)
 
 

time: 51 us -> 47.8 us (0.937)
  Pallas kernels: 48.3 us -> 46.1 us
  other arithmetic: 1.93 us -> 0.89 us
    pallas_call x1, Pallas kernels: 48.3 us -> 46.1 us  [shards(): pl.pallas_call(kernel, out_shape=jax.ShapeDtypeStruct((3, ROWS, GROUP * P...]
    convert_element_type x1, other arithmetic: 1.93 us -> 0.89 us  [shards(): return (r[0].astype(F32), r[1].astype(F32), r[2].astype(F32))]
where the time goes in v4:
time: 47.8 us; the launch traced here: 47.7 us
  Pallas kernels  46.1 us (96%)
  other arithmetic  0.89 us (2%)
  between operations  0.64 us (1%)
    pallas_call x1, Pallas kernels, shards(): pl.pallas_call(kernel, out_shape=jax.ShapeDtypeStruct((3, ROWS, GROUP * P...  46.1 us

profile of v4, /device:TPU:1, one launch (start us, length us, event | category | flops | bytes accessed | tf_op | source)
XLA Modules:
  0.0 47.7 jit_solution(8175914402654675901)
XLA Ops:
  0.6 46.1 %shard_map.85 = bf16[3,64,1024]{2,1,0:T(8,128)(2,1)S(1)} custom-call(bf16[64,1024]{1,0:T(8,128)(2,1)} %q_hbm.1, bf16[64,1024]{1,0:T(8,128)(2,1)} %k_hbm.1, bf16[64,1024]{1,0:T(8,128)(2,1)} %v_hbm.1, bf16[64,1024]{1,0:T(8,128)(2,1)} %o_hbm.1, bf16[64,1024]{1,0:T(8,128)(2,1)} %g_hbm.1, f32[16,64]{1,0:T(8,128)} %bitcast.10), custom_call_target="tpu_custom_call" | custom-call | flops 5368709120 | bytes 2097152 | tf_op jit(solution)/shard_map/pallas_call | solution.py:439
  46.8 0.9 %bitcast_convert_fusion = (f32[64,1024]{1,0:T(8,128)}, f32[64,1024]{1,0:T(8,128)}, f32[64,1024]{1,0:T(8,128)}) fusion(bf16[3,64,1024]{2,1,0:T(8,128)(2,1)S(1)} %shard_map.85), kind=kLoop, calls=%fused_computation | loop fusion | flops 196608 | bytes 1179648 | tf_op jit(solution)/shard_map/convert_element_type | solution.py:482

commit v5 on v4

--- a/solution.py
+++ b/solution.py
@@ -19,13 +19,9 @@
 OFFSETS = (0, 1, -1, 2)
 SLOT_AT = {1: 2, -1: 1, 2: 3}
 FAR = (1, 2, 3)
-STEPS = RING * RING
-TILES = (
-    (0, 0), (1, 0), (1, 1), (2, 0), (2, 1), (2, 2), (1, 2), (1, 3),
-    (2, 3), (0, 3), (3, 3), (3, 0), (3, 1), (3, 2), (0, 1), (0, 2),
-)
-FORWARD_AT = {2: 1, 3: 2}
-HOP_AFTER = 5
+WHOLE = (0, CHUNK)
+NEAR = (0, 2 * ROWS)
+REST = (2 * ROWS, CHUNK)
 
 
 def dot_nn(a, b):
@@ -259,34 +255,41 @@
     qbuf[0, 0] = stage_q[me]
 
     pl.semaphore_wait(barrier, 19)
+    for offset in (-1, 1):
+        for other in (0, 1):
+            cross_copy(1, offset, other).start()
+            cross_copy(0, offset, other).start()
     for offset, other in near:
         near_copy(1, offset, other).start()
         near_copy(0, offset, other).start()
-    for offset in (1, -1):
-        for other in (0, 1):
-            cross_copy(1, offset, other).start()
-            cross_copy(0, offset, other).start()
     dq_acc[...] = jnp.zeros_like(dq_acc)
     dk_acc[...] = jnp.zeros_like(dk_acc)
     dv_acc[...] = jnp.zeros_like(dv_acc)
 
     lane = lax.broadcasted_iota(jnp.int32, (1, PAIR), 1)
 
-    def prepare_q(slot):
-        q = qbuf[slot, :, 0:ROWS, :].reshape(CHUNK, PAIR)
-        g = qbuf[slot, :, ROWS : 2 * ROWS, :].reshape(CHUNK, PAIR)
+    def prepare_q(chunk, rows):
+        first, last = rows
+        pieces = slice(first // ROWS, last // ROWS)
+        q = qbuf[chunk, pieces, 0:ROWS, :].reshape(last - first, PAIR)
+        g = qbuf[chunk, pieces, ROWS : 2 * ROWS, :].reshape(last - first, PAIR)
         for h in range(2):
             own = jnp.where(lane // HEAD == h, 1.0, 0.0)
-            qm[slot, h] = q * (own * HEAD**-0.5).astype(BF)
-            gm[slot, h] = g * own.astype(BF)
-        for i in range(RING):
-            part = qbuf[slot, 2 * i, 2 * ROWS : SIDE, :].astype(F32)
-            part += qbuf[slot, 2 * i + 1, 2 * ROWS : SIDE, :].astype(F32)
-            terms[slot, 0:4, i * PAIR : (i + 1) * PAIR] = part[0:4] + part[4:8] + part[8:12]
-
-    def prepare_k(slot):
-        k = kbuf[slot, :, 0:ROWS, :].reshape(CHUNK, PAIR).astype(F32)
-        kt[slot] = (k * HEAD**-0.5).T.astype(BF)
+            qm[chunk, h, first:last] = q * (own * HEAD**-0.5).astype(BF)
+            gm[chunk, h, first:last] = g * own.astype(BF)
+        for i in range(first // PAIR, last // PAIR):
+            part = qbuf[chunk, 2 * i, 2 * ROWS : SIDE, :].astype(F32)
+            part += qbuf[chunk, 2 * i + 1, 2 * ROWS : SIDE, :].astype(F32)
+            terms[chunk, 0:4, i * PAIR : (i + 1) * PAIR] = part[0:4] + part[4:8] + part[8:12]
+
+    def keys(chunk, rows, low, high):
+        first, last = rows
+        pieces = slice(first // ROWS, last // ROWS)
+        return kbuf[chunk, pieces, low:high, :].reshape(last - first, PAIR)
+
+    def prepare_k(chunk, rows):
+        k = keys(chunk, rows, 0, ROWS).astype(F32)
+        kt[chunk, :, rows[0] : rows[1]] = (k * HEAD**-0.5).T.astype(BF)
 
     def pass_on(chunk):
         for side in (1, 0):
@@ -294,30 +297,46 @@
             for offset in OFFSETS[1:]:
                 ring_copy(side, chunk, offset).start()
 
-    def arrive(side, chunk):
-        (near_all(side) if chunk == 0 else ring_all(side, chunk)).wait_recv()
-        (prepare_q, prepare_k)[side](chunk)
+    def arrive(side, chunk, rows=REST):
+        (ring_all(side, chunk) if chunk else near_all(side)).wait_recv()
+        (prepare_q, prepare_k)[side](chunk, rows)
 
     pass_on(1)
     for other in (0, 1):
         cross_copy(1, 2, other).start()
         cross_copy(0, 2, other).start()
-    arrive(1, 0)
-    arrive(0, 0)
-
-    def tile(kslot, qslot):
-        k = kbuf[kslot, :, 0:ROWS, :].reshape(CHUNK, PAIR)
-        v = kbuf[kslot, :, ROWS : 2 * ROWS, :].reshape(CHUNK, PAIR)
+    arrive(1, 0, WHOLE)
+    arrive(0, 0, WHOLE)
+
+    def join(parts, axis):
+        return parts[0] if len(parts) == 1 else jnp.concatenate(parts, axis=axis)
+
+    def tile(key_parts, query_parts):
+        k = join([keys(chunk, rows, 0, ROWS) for chunk, rows in key_parts], 0)
+        v = join([keys(chunk, rows, ROWS, 2 * ROWS) for chunk, rows in key_parts], 0)
         for h in range(2):
-            q = qm[qslot, h]
-            g = gm[qslot, h]
-            probs = jnp.exp(dot_nt(k, q) - terms[qslot, h : h + 1, :])
-            grad = probs * (dot_nt(v, g) - terms[qslot, 2 + h : 3 + h, :])
-            grad = grad.astype(BF)
-            dv_acc[kslot] += dot_nn(probs.astype(BF), g)
-            dk_acc[kslot] += dot_nn(grad, q)
-            rows = slice(h * HEAD, (h + 1) * HEAD)
-            dq_acc[qslot, rows, :] += dot_nn(kt[kslot, rows, :], grad)
+            head = slice(h * HEAD, (h + 1) * HEAD)
+            q = join([qm[c, h, a:b] for c, (a, b) in query_parts], 0)
+            g = join([gm[c, h, a:b] for c, (a, b) in query_parts], 0)
+            sums = join([terms[c, h : h + 1, a:b] for c, (a, b) in query_parts], 1)
+            delta = join([terms[c, 2 + h : 3 + h, a:b] for c, (a, b) in query_parts], 1)
+            probs = jnp.exp(dot_nt(k, q) - sums)
+            grad = (probs * (dot_nt(v, g) - delta)).astype(BF)
+            dv = dot_nn(probs.astype(BF), g)
+            dk = dot_nn(grad, q)
+            dq = dot_nn(join([kt[c, head, a:b] for c, (a, b) in key_parts], 1), grad)
+            at = 0
+            for c, (a, b) in key_parts:
+                dv_acc[c, a:b] += dv[at : at + b - a]
+                dk_acc[c, a:b] += dk[at : at + b - a]
+                at += b - a
+            at = 0
+            for c, (a, b) in query_parts:
+                dq_acc[c, head, a:b] += dq[:, at : at + b - a]
+                at += b - a
+
+    def whole(kslot, qslot):
+        tile([(kslot, WHOLE)], [(qslot, WHOLE)])
 
     half = 2 * ROWS
 
@@ -341,53 +360,64 @@
         for other in (0, 1):
             back_copy(chunk, other).start()
 
-    def send_direct():
-        for piece in range(1, GROUP):
+    def send_direct(pieces):
+        for piece in pieces:
             rows = slice(piece * ROWS, (piece + 1) * ROWS)
             near_kv[piece, 0] = dk_acc[0, rows].astype(BF)
             near_kv[piece, 1] = dv_acc[0, rows].astype(BF)
-        for offset, other in near:
-            direct_copy(offset, other).start()
-
-    def send_query(chunk):
-        total = dq_acc[chunk].T
-        if not chunk:
+        for piece in reversed(pieces):
+            direct_copy(OFFSETS[piece // 2], piece % 2).start()
+
+    def send_query(chunk, pieces):
+        first, last = pieces[0] * ROWS, (pieces[-1] + 1) * ROWS
+        total = dq_acc[chunk, :, first:last].T
+        if chunk == 0:
             own_q[...] = total[0:ROWS]
-        send_q[chunk] = total.astype(BF).reshape(GROUP, ROWS, PAIR)
-        for offset, other in near + [(0, 0)] * bool(chunk):
-            query_copy(chunk, offset, other).start()
-
-    events = {}
-    for chunk, i in FORWARD_AT.items():
-        events.setdefault(i, []).append((pass_on, (chunk,)))
-    seen = {(0, 0), (1, 0)}
-    left = {(side, chunk): RING for side in range(2) for chunk in range(RING)}
-    for i, order in enumerate(TILES):
-        for side in (1, 0):
-            chunk = order[1 - side]
-            if (side, chunk) not in seen:
-                seen.add((side, chunk))
-                events.setdefault(i, []).append((arrive, (side, chunk)))
-            left[side, chunk] -= 1
-            if not left[side, chunk]:
-                if not side:
-                    events.setdefault(i + 1, []).append((send_query, (chunk,)))
-                elif chunk:
-                    events.setdefault(i + 1, []).append((send_sums, (chunk,)))
-                    after = min(i + 1 + HOP_AFTER, STEPS + 1)
-                    events.setdefault(after, []).append((hop, (chunk,)))
-                else:
-                    events.setdefault(i + 1, []).append((send_direct, ()))
-
-    def run(i):
-        for act, operands in events.get(i, []):
-            act(*operands)
-
-    for i, order in enumerate(TILES):
-        run(i)
-        tile(*order)
-    run(STEPS)
-    run(STEPS + 1)
+        total = total.astype(BF).reshape(len(pieces), ROWS, PAIR)
+        send_q[chunk, pieces[0] : pieces[-1] + 1] = total
+        for piece in reversed(pieces):
+            if chunk or piece:
+                query_copy(chunk, OFFSETS[piece // 2], piece % 2).start()
+
+    whole(0, 0)
+    pass_on(2)
+    for chunk in (1, 2):
+        prepare_k(chunk, NEAR)
+        prepare_q(chunk, NEAR)
+    tile([(1, NEAR), (2, NEAR)], [(0, WHOLE)])
+    arrive(1, 1)
+    tile([(1, REST)], [(0, WHOLE)])
+    pass_on(3)
+    arrive(0, 1)
+    whole(1, 1)
+    arrive(1, 2)
+    tile([(2, REST)], [(0, WHOLE)])
+    whole(2, 1)
+    arrive(0, 2)
+    whole(2, 2)
+    whole(1, 2)
+    arrive(0, 3, WHOLE)
+    whole(1, 3)
+    send_sums(1)
+    whole(2, 3)
+    send_sums(2)
+    whole(0, 3)
+    arrive(1, 3, WHOLE)
+    whole(3, 3)
+    send_query(3, range(8))
+    whole(3, 0)
+    send_query(0, range(8))
+    whole(3, 1)
+    whole(3, 2)
+    send_sums(3)
+    hop(1)
+    whole(0, 1)
+    send_query(1, range(8))
+    hop(2)
+    whole(0, 2)
+    send_direct(range(1, 8))
+    send_query(2, range(8))
+    hop(3)
 
     def columns(offset, other):
         return pl.ds(pl.multiple_of(pair_at(offset, other) * PAIR, PAIR), PAIR)
@@ -396,6 +426,17 @@
         for part in parts:
             first = first + part.astype(F32)
         return first.astype(BF)
+
+    for side in range(2):
+        near_all(side).wait_send()
+        for chunk in FAR:
+            cross_all(side, chunk).wait_send()
+            ring_all(side, chunk).wait_send()
+    for chunk in (0, 1, 3):
+        query_all(chunk).wait_send()
+    for chunk in FAR:
+        sum_all(chunk).wait_send()
+    back_all().wait_send()
 
     back_all().wait_recv()
     for chunk in FAR:
@@ -416,18 +457,8 @@
             parts = [direct_kv[2 * slot + other, i] for slot in range(RING)]
             first = parts[0].astype(F32) if other else acc[0, 0:ROWS]
             out_ref[1 + i, :, columns(0, other)] = own_sum(first, parts[1:])
-
-    back_all().wait_send()
     direct_all().wait_send()
-    for chunk in range(RING):
-        query_all(chunk).wait_send()
-    for chunk in FAR:
-        sum_all(chunk).wait_send()
-    for side in range(2):
-        near_all(side).wait_send()
-        for chunk in FAR:
-            cross_all(side, chunk).wait_send()
-            ring_all(side, chunk).wait_send()
+    query_all(2).wait_send()
 
 
 def shards(queries, key_rows, value_rows, output_rows, grad_out, log_sums):

time: 47.8 us -> 47.5 us (level)
  no operation moved by 1% of the time
where the time goes in v5:
time: 47.5 us; the launch traced here: 47.3 us
  Pallas kernels  45.8 us (96%)
  other arithmetic  0.89 us (2%)
  between operations  0.64 us (1%)
    pallas_call x1, Pallas kernels, shards(): pl.pallas_call(kernel, out_shape=jax.ShapeDtypeStruct((3, ROWS, GROUP * P...  45.8 us

profile of v5, /device:TPU:1, one launch (start us, length us, event | category | flops | bytes accessed | tf_op | source)
XLA Modules:
  0.0 47.3 jit_solution(9571258298375971489)
XLA Ops:
  0.6 45.8 %shard_map.85 = bf16[3,64,1024]{2,1,0:T(8,128)(2,1)S(1)} custom-call(bf16[64,1024]{1,0:T(8,128)(2,1)} %q_hbm.1, bf16[64,1024]{1,0:T(8,128)(2,1)} %k_hbm.1, bf16[64,1024]{1,0:T(8,128)(2,1)} %v_hbm.1, bf16[64,1024]{1,0:T(8,128)(2,1)} %o_hbm.1, bf16[64,1024]{1,0:T(8,128)(2,1)} %g_hbm.1, f32[16,64]{1,0:T(8,128)} %bitcast.10), custom_call_target="tpu_custom_call" | custom-call | flops 5368709120 | bytes 2097152 | tf_op jit(solution)/shard_map/pallas_call | solution.py:470
  46.4 0.9 %bitcast_convert_fusion = (f32[64,1024]{1,0:T(8,128)}, f32[64,1024]{1,0:T(8,128)}, f32[64,1024]{1,0:T(8,128)}) fusion(bf16[3,64,1024]{2,1,0:T(8,128)(2,1)S(1)} %shard_map.85), kind=kLoop, calls=%fused_computation | loop fusion | flops 196608 | bytes 1179648 | tf_op jit(solution)/shard_map/convert_element_type | solution.py:513

commit v6 on v5

--- a/solution.py
+++ b/solution.py
@@ -162,20 +162,20 @@
         view = bufs[side].at[chunk, afar]
         return remote(view, view, ring_sem, (side, chunk), along_x(0, 1))
 
-    def sum_copy(chunk, offset):
-        return remote(
-            ring_kv.at[chunk, OFFSETS.index(offset)], came_kv.at[chunk, SLOT_AT[offset]],
-            sum_sem, (chunk,), along_z(offset),
-        )
-
-    def sum_all(chunk):
-        view = came_kv.at[chunk, 1:4]
-        return remote(view, view, sum_sem, (chunk,), along_x(0, 1))
-
-    def back_copy(chunk, other):
+    def sum_copy(chunk, offset, i):
+        return remote(
+            ring_kv.at[chunk, i, OFFSETS.index(offset)], came_kv.at[chunk, i, SLOT_AT[offset]],
+            sum_sem, (chunk, i), along_z(offset),
+        )
+
+    def sum_all(chunk, i):
+        view = came_kv.at[chunk, i, 1:4]
+        return remote(view, view, sum_sem, (chunk, i), along_x(0, 1))
+
+    def back_copy(chunk, other, i):
         piece = 2 * chunk + other
         return remote(
-            back_kv.at[piece], home_kv.at[piece],
+            back_kv.at[piece, i], home_kv.at[piece, i],
             back_sem, (), along_x(OFFSETS[chunk], other),
         )
 
@@ -341,24 +341,23 @@
     half = 2 * ROWS
 
     def send_sums(chunk):
-        for slot in FAR:
-            rows = slice(slot * half, (slot + 1) * half)
-            ring_kv[chunk, slot, 0] = dk_acc[chunk, rows].astype(BF)
-            ring_kv[chunk, slot, 1] = dv_acc[chunk, rows].astype(BF)
-        for offset in OFFSETS[1:]:
-            sum_copy(chunk, offset).start()
+        for i, acc in enumerate((dk_acc, dv_acc)):
+            for slot in FAR:
+                rows = slice(slot * half, (slot + 1) * half)
+                ring_kv[chunk, i, slot] = acc[chunk, rows].astype(BF)
+            for offset in OFFSETS[1:]:
+                sum_copy(chunk, offset, i).start()
 
     def hop(chunk):
-        sum_all(chunk).wait_recv()
         for i, acc in enumerate((dk_acc, dv_acc)):
+            sum_all(chunk, i).wait_recv()
             total = acc[chunk, 0:half]
             for slot in FAR:
-                total = total + came_kv[chunk, slot, i].astype(F32)
+                total = total + came_kv[chunk, i, slot].astype(F32)
             for other in (0, 1):
                 rows = slice(other * ROWS, (other + 1) * ROWS)
                 back_kv[2 * chunk + other, i] = total[rows].astype(BF)
-        for other in (0, 1):
-            back_copy(chunk, other).start()
+                back_copy(chunk, other, i).start()
 
     def send_direct(pieces):
         for piece in pieces:
@@ -415,8 +414,8 @@
     send_query(1, range(8))
     hop(2)
     whole(0, 2)
+    send_query(2, range(8))
     send_direct(range(1, 8))
-    send_query(2, range(8))
     hop(3)
 
     def columns(offset, other):
@@ -435,7 +434,8 @@
     for chunk in (0, 1, 3):
         query_all(chunk).wait_send()
     for chunk in FAR:
-        sum_all(chunk).wait_send()
+        for i in range(2):
+            sum_all(chunk, i).wait_send()
     back_all().wait_send()
 
     back_all().wait_recv()
@@ -486,8 +486,8 @@
             pltpu.VMEM((RING, PAIR, CHUNK), F32),
             pltpu.VMEM((RING, CHUNK, PAIR), F32),
             pltpu.VMEM((RING, CHUNK, PAIR), F32),
-            pltpu.VMEM((RING, RING, 2, 2 * ROWS, PAIR), BF),
-            pltpu.VMEM((RING, RING, 2, 2 * ROWS, PAIR), BF),
+            pltpu.VMEM((RING, 2, RING, 2 * ROWS, PAIR), BF),
+            pltpu.VMEM((RING, 2, RING, 2 * ROWS, PAIR), BF),
             pltpu.VMEM((GROUP, 2, ROWS, PAIR), BF),
             pltpu.VMEM((GROUP, 2, ROWS, PAIR), BF),
             pltpu.VMEM((GROUP, 2, ROWS, PAIR), BF),
@@ -498,7 +498,7 @@
             dma((2, 2)),
             dma((2, 2, RING)),
             dma((2, 2, RING)),
-            dma((2, RING)),
+            dma((2, RING, 2)),
             dma((2,)),
             dma((2,)),
             dma((2, RING)),

time: 47.5 us -> 47.3 us (level)
  no operation moved by 1% of the time
where the time goes in v6:
time: 47.3 us; the launch traced here: 47.2 us
  Pallas kernels  45.6 us (96%)
  other arithmetic  0.89 us (2%)
  between operations  0.64 us (1%)
    pallas_call x1, Pallas kernels, shards(): pl.pallas_call(kernel, out_shape=jax.ShapeDtypeStruct((3, ROWS, GROUP * P...  45.6 us

profile of v6, /device:TPU:1, one launch (start us, length us, event | category | flops | bytes accessed | tf_op | source)
XLA Modules:
  0.0 47.2 jit_solution(9142105393262889286)
XLA Ops:
  0.6 45.6 %shard_map.85 = bf16[3,64,1024]{2,1,0:T(8,128)(2,1)S(1)} custom-call(bf16[64,1024]{1,0:T(8,128)(2,1)} %q_hbm.1, bf16[64,1024]{1,0:T(8,128)(2,1)} %k_hbm.1, bf16[64,1024]{1,0:T(8,128)(2,1)} %v_hbm.1, bf16[64,1024]{1,0:T(8,128)(2,1)} %o_hbm.1, bf16[64,1024]{1,0:T(8,128)(2,1)} %g_hbm.1, f32[16,64]{1,0:T(8,128)} %bitcast.10), custom_call_target="tpu_custom_call" | custom-call | flops 5368709120 | bytes 2097152 | tf_op jit(solution)/shard_map/pallas_call | solution.py:470
  46.3 0.9 %bitcast_convert_fusion = (f32[64,1024]{1,0:T(8,128)}, f32[64,1024]{1,0:T(8,128)}, f32[64,1024]{1,0:T(8,128)}) fusion(bf16[3,64,1024]{2,1,0:T(8,128)(2,1)S(1)} %shard_map.85), kind=kLoop, calls=%fused_computation | loop fusion | flops 196608 | bytes 1179648 | tf_op jit(solution)/shard_map/convert_element_type | solution.py:513

commit v7 on v6

--- a/solution.py
+++ b/solution.py
@@ -116,6 +116,7 @@
         for along in (along_x, along_y, along_z)
         for offset in OFFSETS[1:]
         for other in (0, 1)
+        if (along, offset) != (along_x, 2)
     ]:
         pl.semaphore_signal(barrier, inc=1, device_id=peer, device_id_type=MESH)
 
@@ -254,7 +255,7 @@
 
     qbuf[0, 0] = stage_q[me]
 
-    pl.semaphore_wait(barrier, 19)
+    pl.semaphore_wait(barrier, 17)
     for offset in (-1, 1):
         for other in (0, 1):
             cross_copy(1, offset, other).start()

time: 47.3 us -> 47.3 us (level)
  no operation moved by 1% of the time
where the time goes in v7:
time: 47.3 us; the launch traced here: 47.2 us
  Pallas kernels  45.6 us (96%)
  other arithmetic  0.89 us (2%)
  between operations  0.64 us (1%)
    pallas_call x1, Pallas kernels, shards(): pl.pallas_call(kernel, out_shape=jax.ShapeDtypeStruct((3, ROWS, GROUP * P...  45.6 us

profile of v7, /device:TPU:1, one launch (start us, length us, event | category | flops | bytes accessed | tf_op | source)
XLA Modules:
  0.0 47.2 jit_solution(1584616619095724962)
XLA Ops:
  0.6 45.6 %shard_map.85 = bf16[3,64,1024]{2,1,0:T(8,128)(2,1)S(1)} custom-call(bf16[64,1024]{1,0:T(8,128)(2,1)} %q_hbm.1, bf16[64,1024]{1,0:T(8,128)(2,1)} %k_hbm.1, bf16[64,1024]{1,0:T(8,128)(2,1)} %v_hbm.1, bf16[64,1024]{1,0:T(8,128)(2,1)} %o_hbm.1, bf16[64,1024]{1,0:T(8,128)(2,1)} %g_hbm.1, f32[16,64]{1,0:T(8,128)} %bitcast.10), custom_call_target="tpu_custom_call" | custom-call | flops 5368709120 | bytes 2097152 | tf_op jit(solution)/shard_map/pallas_call | solution.py:471
  46.3 0.9 %bitcast_convert_fusion = (f32[64,1024]{1,0:T(8,128)}, f32[64,1024]{1,0:T(8,128)}, f32[64,1024]{1,0:T(8,128)}) fusion(bf16[3,64,1024]{2,1,0:T(8,128)(2,1)S(1)} %shard_map.85), kind=kLoop, calls=%fused_computation | loop fusion | flops 196608 | bytes 1179648 | tf_op jit(solution)/shard_map/convert_element_type | solution.py:514
